TPU v7x, 32 devices: a whole 2x2x4 slice. The times are simulated.
32 devices in a mesh: ctx: 8 (over z, y), head: 4 (over x, core).
Axes of the slice: x: 2, y: 2, z: 4, core: 2. Of those that a mesh axis runs over, the one named last changes fastest.
Arguments:
- tokens: bfloat16 [4096, 2560], P('ctx', 'head'), may hold values from -6 to 6
- tangent_tokens: bfloat16 [4096, 2560], P('ctx', 'head'), may hold values from -6 to 6
- log_decay: float32 [4096, 80], P('ctx', 'head'), may hold values from -1.5 to 0, as said below
- tangent_decay: float32 [4096, 80], P('ctx', 'head'), may hold values from -0.096 to 0.096
- w_inner: bfloat16 [2560, 5120], P(None, 'head'), may hold values from -0.125 to 0.125
- w_bmat: bfloat16 [2560, 128], replicated, may hold values from -0.00390625 to 0.00390625
- w_cmat: bfloat16 [2560, 128], replicated, may hold values from -0.125 to 0.125
- conv_inner: float32 [4, 5120], P(None, 'head'), may hold values from -3 to 3
- conv_bc: float32 [4, 256], replicated, may hold values from -3 to 3
- skip_gain: float32 [80], P('head'), may hold values from 0.5 to 2
- w_out: bfloat16 [5120, 2560], P('head'), may hold values from -0.078125 to 0.078125
Outputs:
- output: bfloat16 [4096, 2560], P('ctx', 'head')
- output_tangent: bfloat16 [4096, 2560], P('ctx', 'head')
Inputs may be any that keep to these rules, and one draw needn't show every extreme that they name: `log_decay`: negative; the natural logarithm of the factor by which each head's state is multiplied at each token.
All inputs are finite; a program needn't handle non-finite values.
Results may differ from a plain program's by a relative error of at most 0.019.
Values may be sent and summed in bfloat16 or wider, within the bound.
A program may use at most 128 MiB of HBM per device.

v0:
```python
import jax
import jax.numpy as jnp
from jax import lax
from jax.sharding import PartitionSpec as P

HEAD_DIM = 64
SPAN = 256


def shifted(block, axis, distance):
    devices = range(lax.axis_size(axis))
    route = [(i - distance, i) for i in devices if i - distance in devices]
    return lax.ppermute(block, axis, route)


def carried_in(part, axis, combine, identity):
    place = lax.axis_index(axis)
    gathered = jax.tree.map(lambda a: lax.all_gather(a, axis), part)
    state = jax.tree.map(lambda a, e: jnp.zeros_like(a) + jnp.asarray(e, a.dtype), part, identity)

    def one(step, state):
        return combine(
            state, jax.tree.map(lambda a: lax.dynamic_index_in_dim(a, step, 0, False), gathered)
        )

    return lax.fori_loop(0, place, one, state)


def depthwise(padded, kernel):
    length = padded.shape[0] - kernel.shape[0] + 1
    summed = kernel[0] * padded[0:length]
    for offset in range(1, kernel.shape[0]):
        summed = summed + kernel[offset] * padded[offset : offset + length]
    return summed


def activate(values):
    return jax.nn.silu(values).astype(jnp.bfloat16)


def span_parts(inputs, writer, reader, decays):
    cumulative = jnp.cumsum(decays, axis=0)
    length = decays.shape[0]
    causal = lax.broadcasted_iota(jnp.int32, (length, length), 0) >= lax.broadcasted_iota(
        jnp.int32, (length, length), 1
    )
    differences = cumulative.T[:, :, None] - cumulative.T[:, None, :]
    weights = jnp.exp(jnp.where(causal[None], differences, -jnp.inf))
    scores = jnp.dot(reader, writer.T, preferred_element_type=jnp.float32)
    mixing = (weights * scores[None]).astype(jnp.bfloat16)
    within = jnp.einsum("hts,shp->thp", mixing, inputs, preferred_element_type=jnp.float32)
    remaining = jnp.exp(cumulative[-1][None, :] - cumulative)
    scaled = (inputs * remaining[:, :, None]).astype(jnp.bfloat16)
    block_state = jnp.einsum("shp,sn->hpn", scaled, writer, preferred_element_type=jnp.float32)
    return (cumulative, within, block_state)


def carried(reader, cumulative, initial):
    readout = jnp.einsum(
        "tn,hpn->thp", reader, initial.astype(jnp.bfloat16), preferred_element_type=jnp.float32
    )
    return jnp.exp(cumulative)[:, :, None] * readout


def combine(earlier, later):
    early_total, early_slope, early_state, early_tangent = earlier
    late_total, late_slope, late_state, late_tangent = later
    retain = jnp.exp(late_total)
    return (
        early_total + late_total,
        early_slope + late_slope,
        retain * early_state + late_state,
        retain * (early_tangent + late_slope * early_state) + late_tangent,
    )


def on_device(
    tokens,
    tangent_tokens,
    log_decay,
    tangent_decay,
    w_inner,
    w_bmat,
    w_cmat,
    conv_inner,
    conv_bc,
    skip_gain,
    w_out,
):
    length = tokens.shape[0]
    width = w_inner.shape[1]
    state_len = w_bmat.shape[1]
    heads_here = width // HEAD_DIM
    margin = conv_inner.shape[0] - 1
    blocks = length // SPAN
    stacked = jnp.concatenate([tokens, tangent_tokens], 0)
    shard_piece = lax.all_gather(stacked, "head", axis=1, tiled=True)
    sums = (
        jnp.dot(shard_piece, w_inner, preferred_element_type=jnp.float32),
        jnp.dot(shard_piece, w_bmat, preferred_element_type=jnp.float32),
        jnp.dot(shard_piece, w_cmat, preferred_element_type=jnp.float32),
    )
    projected = jnp.concatenate([summand.astype(jnp.bfloat16) for summand in sums], 1)
    edges = jnp.stack([projected[length - margin : length], projected[2 * length - margin :]])
    previous = shifted(edges, "ctx", 1)
    kernel = jnp.concatenate([conv_inner, conv_bc], 1)
    primal_conv = depthwise(jnp.concatenate([previous[0], projected[:length]], 0), kernel)
    tangent_conv = depthwise(jnp.concatenate([previous[1], projected[length:]], 0), kernel)
    mixed, mixed_dot = jax.jvp(activate, (primal_conv,), (tangent_conv,))

    def separate(values):
        inputs = values[:, :width].reshape(blocks, SPAN, heads_here, HEAD_DIM)
        writer = values[:, width : width + state_len].reshape(blocks, SPAN, state_len)
        reader = values[:, width + state_len :].reshape(blocks, SPAN, state_len)
        return (inputs, writer, reader)

    inputs, writer, reader = separate(mixed)
    inputs_dot, writer_dot, reader_dot = separate(mixed_dot)
    decays = log_decay.reshape(blocks, SPAN, heads_here)
    decays_dot = tangent_decay.reshape(blocks, SPAN, heads_here)
    (cumulative, within, block_state), (cumulative_dot, within_dot, block_dot) = jax.jvp(
        jax.vmap(span_parts),
        (inputs, writer, reader, decays),
        (inputs_dot, writer_dot, reader_dot, decays_dot),
    )

    def summarize(cumulative, block_state):
        summed = cumulative[0, -1]
        running = block_state[0]
        summed = summed + cumulative[1, -1]
        running = jnp.exp(cumulative[1, -1])[:, None, None] * running + block_state[1]
        return (summed[:, None, None], running)

    (decay_sum, own_state), (decay_sum_dot, own_dot) = jax.jvp(
        summarize, (cumulative, block_state), (cumulative_dot, block_dot)
    )
    message = (decay_sum, decay_sum_dot, own_state, own_dot)
    empty = tuple((jnp.zeros_like(member) for member in message))
    arriving = carried_in(message, "ctx", combine, empty)
    entry_state = arriving[2]
    entry_dot = arriving[3]

    def finish(initial, cumulative, within, block_state, inputs, reader):
        outputs = []
        for position in range(cumulative.shape[0]):
            combined = (
                within[position]
                + carried(reader[position], cumulative[position], initial)
                + skip_gain[None, :, None] * inputs[position]
            )
            outputs.append(combined.astype(jnp.bfloat16))
            if position + 1 < cumulative.shape[0]:
                initial = (
                    jnp.exp(cumulative[position, -1])[:, None, None] * initial
                    + block_state[position]
                )
        return jnp.stack(outputs)

    inner, inner_dot = jax.jvp(
        finish,
        (entry_state, cumulative, within, block_state, inputs, reader),
        (entry_dot, cumulative_dot, within_dot, block_dot, inputs_dot, reader_dot),
    )
    flattened = jnp.concatenate([inner.reshape(length, width), inner_dot.reshape(length, width)], 0)
    partial_term = jnp.dot(flattened, w_out, preferred_element_type=jnp.float32).astype(
        jnp.bfloat16
    )
    summed = (
        lax.psum_scatter(partial_term, "head", scatter_dimension=1, tiled=True)
        .astype(jnp.float32)
        .astype(jnp.bfloat16)
    )
    return (summed[:length], summed[length:])


def solution(mesh):
    in_specs = (
        P("ctx", "head"),
        P("ctx", "head"),
        P("ctx", "head"),
        P("ctx", "head"),
        P(None, "head"),
        P(),
        P(),
        P(None, "head"),
        P(),
        P("head"),
        P("head", None),
    )
    out_specs = (P("ctx", "head"), P("ctx", "head"))
    return jax.shard_map(
        on_device, mesh=mesh, in_specs=in_specs, out_specs=out_specs, check_vma=False
    )
```

profile of v0, /device:TPU:28, one launch (start us, length us, event | category | flops | bytes accessed | tf_op | source)
XLA Modules:
  0.0 374.4 jit_solution(16632167913559238653)
XLA Ops:
  7.3 2.5 pad_maximum_fusion.3
  10.0 1.2 reduce-window.14
  11.9 1.2 reduce-window.16
  13.4 0.7 slice_reduce_fusion.4
  14.1 1.0 exponential_reduce_fusion
  16.4 0.7 subtract_multiply_fusion.1
  17.1 34.2 %all-gather.6.cloned.1.call-done = bf16[1024,2560]{1,0:T(8,128)(2,1)} async-done(((bf16[1024,640]{1,0:T(8,128)(2,1)}), bf16[1024,2560]{1,0:T(8,128)(2,1)}) %all-gather.6.cloned.1.call-update) | async-done | bytes 5242896 | tf_op jit(solution)/shard_map/all_gather | solution.py:97
  51.3 10.9 %convolution_convert_fusion.1 = bf16[1024,1280]{1,0:T(8,128)(2,1)S(1)} fusion(bf16[1024,2560]{1,0:T(8,128)(2,1)} %all-gather.6.cloned.1.call-done, bf16[2560,1280]{1,0:T(8,128)(2,1)} %param.17), kind=kOutput, calls=%fused_computation.34 | convolution fusion | flops 6712197120 | bytes 14417920 | tf_op jit(solution)/shard_map/dot_general | solution.py:99
  62.3 1.5 convolution_convert_fusion.2
  63.8 1.5 convolution_convert_fusion.3
  65.7 1.5 collective-permute-start
  67.3 4.0 %collective-permute-done = bf16[2,3,1536]{2,1,0:T(4,128)(2,1)S(1)} collective-permute-done((bf16[2,3,1536]{2,1,0:T(4,128)(2,1)S(1)}, bf16[2,3,1536]{2,1,0:T(4,128)(2,1)S(1)}, u32[]{:S(2)}, u32[]{:S(2)}) %collective-permute-start) | collective-permute-done | bytes 18464 | tf_op jit(solution)/shard_map/ppermute | solution.py:13
  71.4 2.2 multiply_convert_fusion.3
  73.6 1.2 slice.252
  74.8 2.7 fusion.28
  77.5 1.2 slice.275
  79.4 2.4 copy.154
  81.8 4.0 %reshape.236 = bf16[2,256,20,64]{1,0,3,2:T(2,128)(2,1)} reshape(bf16[512,1280]{0,1:T(8,128)(2,1)} %copy.154) | data formatting | bytes 2621440 | tf_op jit(solution)/shard_map/reshape | solution.py:112
  85.9 2.4 copy.138
  88.3 4.0 %reshape.227 = bf16[2,256,20,64]{1,0,3,2:T(2,128)(2,1)} reshape(bf16[512,1280]{0,1:T(8,128)(2,1)} %copy.138) | data formatting | bytes 2621440 | tf_op jit(solution)/shard_map/reshape | solution.py:112
  92.4 2.0 fusion.65
  95.6 1.1 copy-done.3
  96.7 1.3 slice_add_fusion
  98.8 1.4 copy.141
  100.2 1.3 copy.145
  101.5 1.3 copy.146
  104.6 16.2 %all-gather = f32[8,1,20]{2,1,0:T(1,128)S(1)} all-gather(f32[1,1,20]{2,1,0:T(1,128)S(1)} %add.124), channel_id=2, replica_groups=mesh['ctx'=8,'head'=4] {'ctx'}, dimensions={0}, use_global_device_ids=true | all-gather | bytes 720 | tf_op jit(solution)/shard_map/all_gather | solution.py:18
  120.8 18.9 %all-gather.1 = f32[8,1,20]{2,1,0:T(1,128)S(1)} all-gather(f32[1,1,20]{2,1,0:T(1,128)} %copy.153), channel_id=3, replica_groups=mesh['ctx'=8,'head'=4] {'ctx'}, dimensions={0}, use_global_device_ids=true | all-gather | bytes 720 | tf_op jit(solution)/shard_map/all_gather | solution.py:18
  140.3 0.8 slice_exponential_fusion.1
  141.1 1.4 fusion.88
  142.4 1.4 fusion.87
  143.8 1.7 slice_convert_fusion.3
  145.5 2.8 copy.158
  148.3 2.9 copy.159
  151.2 1.7 slice_convert_fusion.1
  152.9 2.8 copy.165
  155.7 2.9 copy.166
  159.4 4.1 %fusion.35 = f32[2,256,20,64]{1,3,2,0:T(8,128)} fusion(f32[2,256,256]{2,1,0:T(8,128)S(1)} %fusion.98, f32[2,20,256]{2,1,0:T(8,128)S(1)} %copy-done.28, pred[256,256]{1,0:T(8,128)(4,1)S(1)} %copy-done.25, bf16[2,256,20,64]{1,0,3,2:T(2,128)(2,1)S(1)} %copy-done.9), kind=kOutput, calls=%fused_computation.56 | convolution fusion | flops 346030080 | bytes 4562944 | tf_op jit(solution)/shard_map/jvp(vmap(hts,shp->thp))/dot_general | solution.py:51
  163.5 4.4 %fusion.5 = f32[2,20,64,256]{3,2,1,0:T(8,128)S(1)} fusion(f32[2,256,256]{2,1,0:T(8,128)S(1)} %convolution_add_fusion.3, f32[2,20,256]{2,1,0:T(8,128)S(1)} %copy-done.18, f32[2,256,256]{2,1,0:T(8,128)S(1)} %fusion.98, f32[2,20,256]{2,1,0:T(8,128)S(1)} %copy-done.28, pred[256,256]{1,0:T(8,128)(4,1)S(1)} %copy-done.25, bf16[2,256,20,64]{1,0,3,2:T(2,128)(2,1)S(1)} %copy-done.9), kind=kOutput, calls=%fused_computation.13 | convolution fusion | flops 359137280 | bytes 5128192 | tf_op jit(solution)/shard_map/jvp(vmap(hts,shp->thp))/dot_general | solution.py:51
  167.9 4.2 %add_bitcast_fusion = f32[2,256,20,64]{1,3,2,0:T(8,128)} fusion(f32[2,20,64,256]{3,2,1,0:T(8,128)S(1)} %fusion.5, f32[2,256,256]{2,1,0:T(8,128)S(1)} %fusion.98, f32[2,20,256]{2,1,0:T(8,128)S(1)} %copy-done.28, pred[256,256]{1,0:T(8,128)(4,1)S(1)} %copy-done.25, bf16[2,256,20,64]{1,0,3,2:T(2,128)(2,1)S(1)} %copy-done.15), kind=kOutput, calls=%fused_computation.51 | convolution fusion | flops 346685440 | bytes 7184384 | tf_op jit(solution)/shard_map/jvp(vmap(hts,shp->thp))/dot_general | solution.py:51
  172.1 9.6 %all-gather.10.cloned.1.call-done = f32[8,20,64,128]{3,2,1,0:T(8,128)} async-done(((f32[1,20,64,128]{3,2,1,0:T(8,128)}), f32[8,20,64,128]{3,2,1,0:T(8,128)}) %all-gather.10.cloned.1.call-update) | async-done | bytes 5242896 | tf_op jit(solution)/shard_map/all_gather | solution.py:18
  181.7 87.2 %all-gather.8.cloned.1.call-done = f32[8,20,64,128]{3,2,1,0:T(8,128)} async-done(((f32[1,20,64,128]{3,2,1,0:T(8,128)}), f32[8,20,64,128]{3,2,1,0:T(8,128)}) %all-gather.8.cloned.1.call-update) | async-done | bytes 5242896 | tf_op jit(solution)/shard_map/all_gather | solution.py:18
  269.1 13.4 %while.16 = (s32[]{:T(128)}, f32[20,64,128]{2,1,0:T(8,128)S(1)}, f32[20,64,128]{2,1,0:T(8,128)S(1)}, s32[]{:T(128)}, f32[8,20,1,1]{1,3,2,0:T(1,128)S(1)}, /*inde...) while((s32[]{:T(128)}, f32[20,64,128]{2,1,0:T(8,128)S(1)}, ...), condition=%wide.region_5.6_spmd, body=%wide.region_4.5_spmd.sunk | while | flops 983045 | bytes 3932791 | solution.py:26
  269.1 1.8 bitcast_add_fusion.5
  271.0 1.8 bitcast_add_fusion.5
  272.9 1.8 bitcast_add_fusion.5
  274.8 1.8 bitcast_add_fusion.5
  276.6 1.8 bitcast_add_fusion.5
  278.5 1.8 bitcast_add_fusion.5
  280.4 1.8 bitcast_add_fusion.5
  282.8 1.2 fusion.75
  284.1 1.3 fusion.80
  285.8 1.2 fusion.84
  287.0 1.1 fusion.72
  288.3 1.4 copy.160
  291.0 0.7 copy-done.4
  292.1 0.7 fusion.61
  292.9 1.4 copy.167
  294.6 9.3 %convolution_convert_fusion = bf16[1024,2560]{1,0:T(8,128)(2,1)} fusion(bf16[1280,2560]{1,0:T(8,128)(2,1)S(1)} %bitcast.207, bf16[512,1280]{0,1:T(8,128)(2,1)S(1)} %bitcast.184, bf16[512,1280]{0,1:T(8,128)(2,1)S(1)} %bitcast.182), kind=kOutput, calls=%fused_computation.10 | convolution fusion | flops 6718750720 | bytes 14417920 | tf_op jit(solution)/shard_map/dot_general | solution.py:165
  303.9 7.9 %copy.172 = bf16[1024,2560]{0,1:T(8,128)(2,1)} copy(bf16[1024,2560]{1,0:T(8,128)(2,1)} %convolution_convert_fusion) | data formatting | bytes 10485760
  311.9 52.4 %reduce-scatter.4.cloned.1.call-done = bf16[640,1024]{1,0:T(8,128)(2,1)} async-done(((bf16[2560,1024]{1,0:T(8,128)(2,1)}), bf16[640,1024]{1,0:T(8,128)(2,1)}) %reduce-scatter.4.cloned.1.call-update) | async-done | bytes 1310736
  364.3 1.4 fusion.97
  365.7 1.1 copy.177
  366.8 1.1 copy.178
  (144 shorter events, 12.0 us)
Async XLA Ops:
  7.2 55.1 %copy-start = (bf16[2560,128]{1,0:T(8,128)(2,1)S(1)}, bf16[2560,128]{1,0:T(8,128)(2,1)}, u32[]{:S(2)}) copy-start(bf16[2560,128]{1,0:T(8,128)(2,1)} %param.19) | copy-start | bytes 1966084
  7.2 2.7 copy-start.26
  7.2 4.6 %copy-start.27 = (f32[512,20]{0,1:T(8,128)S(1)}, f32[512,20]{0,1:T(8,128)}, u32[]{:S(2)}) copy-start(f32[512,20]{0,1:T(8,128)} %param.16) | copy-start | bytes 122884
  7.2 8.9 %copy-start.30 = (f32[4,1280]{1,0:T(4,128)S(1)}, f32[4,1280]{1,0:T(4,128)}, u32[]{:S(2)}) copy-start(f32[4,1280]{1,0:T(4,128)} %param.20) | copy-start | bytes 61444
  7.2 8.9 %copy-start.32 = (f32[4,256]{1,0:T(4,128)S(1)}, f32[4,256]{1,0:T(4,128)}, u32[]{:S(2)}) copy-start(f32[4,256]{1,0:T(4,128)} %param.21) | copy-start | bytes 12292
  7.2 44.1 %all-gather.6.cloned.1.call-start = ((), (), s32[]{:S(2)}) async-start(), calls=%async_computation.1 | async-start | bytes 6553600 | tf_op jit(solution)/shard_map/all_gather | solution.py:97
  9.8 171.9 %all-gather.10.cloned.1.call-start = ((), (), s32[]{:S(2)}) async-start(), calls=%async_computation.3 | async-start | bytes 5898240 | tf_op jit(solution)/shard_map/all_gather | solution.py:18
  11.6 39.8 %copy-start.16 = (f32[2,20,256]{2,0,1:T(2,128)}, f32[2,20,256]{2,0,1:T(2,128)S(1)}, u32[]{:S(2)}) copy-start(f32[2,20,256]{2,0,1:T(2,128)S(1)} %reduce_window_sum.43) | copy-start | bytes 122884
  13.4 37.9 %copy-start.17 = (f32[2,20,256]{2,1,0:T(8,128)}, f32[2,20,256]{2,1,0:T(8,128)S(1)}, u32[]{:S(2)}) copy-start(f32[2,20,256]{2,1,0:T(8,128)S(1)} %reshape.255) | copy-start | bytes 122884
  15.1 0.5 copy-start.33
  51.3 10.9 %copy-start.36 = (bf16[1024,2560]{1,0:T(8,128)(2,1)S(1)}, bf16[1024,2560]{1,0:T(8,128)(2,1)}, u32[]{:S(2)}) copy-start(bf16[1024,2560]{1,0:T(8,128)(2,1)} %all-gather.6.cloned.1.call-done) | copy-start | bytes 15728644
  62.3 1.5 copy-start.37
  65.7 5.7 %collective-permute-start = (bf16[2,3,1536]{2,1,0:T(4,128)(2,1)S(1)}, bf16[2,3,1536]{2,1,0:T(4,128)(2,1)S(1)}, u32[]{:S(2)}, u32[]{:S(2)}) collective-permute-start(bf16[2,3,1536]{2,1,0:T(4,128)(2,1)S(1)} %pad_maximum_fusion.6), channel_id=1, source_target_pairs={{0,4},{4,8},{8,12},{12,16},{16,20},{20,24},{24,28},{1,5},{5,9},{9,... | collective-permute-start | bytes 55304 | tf_op jit(solution)/shard_map/ppermute | solution.py:13
  77.5 73.7 %copy-start.2 = (bf16[512,1536]{1,0:T(8,128)(2,1)}, bf16[512,1536]{1,0:T(8,128)(2,1)S(1)}, u32[]{:S(2)}) copy-start(bf16[512,1536]{1,0:T(8,128)(2,1)S(1)} %fusion.28) | copy-start | bytes 4718596
  92.3 2.0 copy-start.8
  92.3 2.1 copy-start.14
  92.3 2.1 copy-start.22
  92.3 2.1 copy-start.29
  94.3 1.3 copy-start.11
  95.1 1.6 copy-start.34
  95.1 1.6 copy-start.35
  95.6 1.1 copy-start.3
  98.0 170.9 %all-gather.8.cloned.1.call-start = ((), (), s32[]{:S(2)}) async-start(), calls=%async_computation.2 | async-start | bytes 5898240 | tf_op jit(solution)/shard_map/all_gather | solution.py:18
  98.8 265.6 %reduce-scatter.4.cloned.1.call-start = ((), (), s32[]{:S(2)}) async-start(), calls=%async_computation.4 | async-start | bytes 6553600
  152.9 6.0 %copy-start.19 = (bf16[512,128]{1,0:T(8,128)(2,1)S(1)}, bf16[512,128]{1,0:T(8,128)(2,1)}, u32[]{:S(2)}) copy-start(bf16[512,128]{1,0:T(8,128)(2,1)} %get-tuple-element.170) | copy-start | bytes 393220
  155.7 3.6 copy-start.9
  155.7 3.6 copy-start.25
  155.7 3.6 copy-start.28
  159.4 4.1 %copy-start.18 = (f32[2,20,256]{2,1,0:T(8,128)S(1)}, f32[2,20,256]{2,1,0:T(8,128)}, u32[]{:S(2)}) copy-start(f32[2,20,256]{2,1,0:T(8,128)} %copy-done.17) | copy-start | bytes 122884
  163.5 4.4 %copy-start.15 = (bf16[2,256,20,64]{1,0,3,2:T(2,128)(2,1)S(1)}, bf16[2,256,20,64]{1,0,3,2:T(2,128)(2,1)}, u32[]{:S(2)}) copy-start(bf16[2,256,20,64]{1,0,3,2:T(2,128)(2,1)} %reshape.236) | copy-start | bytes 3932164
  284.1 2.9 copy-start.6
  284.1 2.9 copy-start.7
  284.1 2.9 copy-start.12
  284.1 2.9 copy-start.20
  284.1 2.9 copy-start.21
  284.1 2.9 copy-start.31
  288.2 1.7 copy-start.10
  288.3 2.1 copy-start.13
  288.3 2.1 copy-start.23
  290.4 1.3 copy-start.4
  290.4 1.7 copy-start.5
  290.4 1.7 copy-start.24
  290.4 4.2 %slice-start = ((s8[6553600]{0:T(1024)(128)(4,1)}), s8[4194304]{0:T(1024)(128)(4,1)S(1)}, s32[]{:S(2)}) async-start(s8[6553600]{0:T(1024)(128)(4,1)} %bitcast.206), calls=%async_computation.5 | async-start | bytes 8388608
  292.1 2.5 slice-start.1
  364.3 3.6 copy-start.1
Sparse Core Ops, SparseCore 0:
  10.0 41.3 all-gather.5
  98.1 83.5 all-gather.9
  184.5 84.4 all-gather.7
  312.0 52.2 reduce-scatter.3
where the time goes:
time: 377 us; the launch traced here: 374 us
  waiting for transfers between devices  188 us (50%)
  local copies, waits for them, and re-layouts  54.8 us (15%)
  matrix products  44.1 us (12%)
  other arithmetic  35.5 us (9%)
  blocking collectives  35 us (9%)
  between operations  14.5 us (4%)
    all_gather x2, waiting for transfers between devices, carried_in(): gathered = jax.tree.map(lambda a: lax.all_gather(a, axis), part)  96.9 us
    unnamed x5, waiting for transfers between devices  53.2 us
    all_gather x2, blocking collectives, carried_in(): gathered = jax.tree.map(lambda a: lax.all_gather(a, axis), part)  35 us
    all_gather x1, waiting for transfers between devices, on_device(): shard_piece = lax.all_gather(stacked, 'head', axis=1, tiled=True)  34.2 us
    unnamed x86, local copies, waits for them, and re-layouts  14 us
    add x7, other arithmetic, combine(): retain * (early_tangent + late_slope * early_state) + late_tangent  12.8 us
    dot_general x3, matrix products, span_parts(): jnp.einsum('hts,shp->thp', mixing, inputs, preferred_element_type=jnp.flo...  12.7 us
    convert_element_type x4, local copies, waits for them, and re-layouts, finish(): skip_gain[None, :, None] * inputs[position]  11.4 us
  transfers between devices with their start and end apart: 5, of which 5 were waited for; matrix products, arithmetic and copies ran while one was open for 12% of the time, Pallas kernels for 0%

commit v1 on v0

--- a/solution.py
+++ b/solution.py
@@ -1,10 +1,645 @@
+import functools
+
 import jax
 import jax.numpy as jnp
 from jax import lax
+from jax.experimental import pallas as pl
+from jax.experimental.pallas import tpu as pltpu
 from jax.sharding import PartitionSpec as P
 
 HEAD_DIM = 64
 SPAN = 256
+MESH = pl.DeviceIdType.MESH
+HIGHEST = lax.Precision.HIGHEST
+VMEM_LIMIT = 56 * 1024 * 1024
+F32 = jnp.float32
+BF16 = jnp.bfloat16
+
+
+def remote(src, dst, send, recv, device):
+    return pltpu.make_async_remote_copy(
+        src_ref=src, dst_ref=dst, send_sem=send, recv_sem=recv, device_id=device, device_id_type=MESH
+    )
+
+
+def greet(devices):
+    barrier = pltpu.get_barrier_semaphore()
+    for device in devices:
+        pl.semaphore_signal(barrier, inc=1, device_id=device, device_id_type=MESH)
+    pl.semaphore_wait(barrier, len(devices))
+
+
+def lanes(start, size):
+    return pl.ds(pl.multiple_of(start, 128), size)
+
+
+def gather_project_kernel(
+    tok, tan, w_in, w_b, w_c, out,
+    held, acc, weight, w_sem, sib_send, sib_recv, far_send, far_recv, fwd_send, fwd_recv,
+):
+    me = lax.axis_index("head")
+    sib = me + 1 - 2 * lax.rem(me, 2)
+    far = lax.rem(me + 2, 4)
+    far_sib = lax.rem(sib + 2, 4)
+    rows_in, feat = tok.shape
+    width = w_in.shape[1]
+    state = w_b.shape[1]
+    chunk = SPAN
+    per = rows_in // chunk
+    count = 2 * per
+    loads = [
+        pltpu.make_async_copy(w_in, weight.at[:, 0:width], w_sem.at[0]),
+        pltpu.make_async_copy(w_b, weight.at[:, width : width + state], w_sem.at[1]),
+        pltpu.make_async_copy(w_c, weight.at[:, width + state : width + 2 * state], w_sem.at[2]),
+    ]
+    for load in loads:
+        load.start()
+    greet([{"head": sib}, {"head": far}])
+
+    def own(r):
+        ref, at = (tok, r) if r < per else (tan, r - per)
+        return ref.at[at * chunk : (at + 1) * chunk]
+
+    def span(r):
+        return slice(r * chunk, (r + 1) * chunk)
+
+    far_copies = [
+        remote(own(r), held.at[1, span(r)], far_send.at[r], far_recv.at[r], {"head": far})
+        for r in range(count)
+    ]
+    sib_copies = [
+        remote(own(r), held.at[0, span(r)], sib_send.at[r], sib_recv.at[r], {"head": sib})
+        for r in range(count)
+    ]
+    fwd_copies = [
+        remote(held.at[1, span(r)], held.at[2, span(r)], fwd_send.at[r], fwd_recv.at[r], {"head": sib})
+        for r in range(count)
+    ]
+    for r in range(count):
+        far_copies[r].start()
+        sib_copies[r].start()
+    for load in loads:
+        load.wait()
+    tiles = weight.shape[1] // 256
+
+    def block(index):
+        return pl.ds(pl.multiple_of(index * feat, 128), feat)
+
+    for r in range(count):
+        sib_copies[r].wait_recv()
+
+        def near(j, _, r=r):
+            cols = lanes(j * 256, 256)
+            acc[span(r), cols] = jnp.dot(
+                own(r)[...], weight[block(me), cols], preferred_element_type=F32
+            ) + jnp.dot(held[0, span(r), :], weight[block(sib), cols], preferred_element_type=F32)
+            return 0
+
+        lax.fori_loop(0, tiles, near, 0)
+
+    def finish(r):
+        fwd_copies[r].wait_recv()
+
+        def last(j, _):
+            cols = lanes(j * 256, 256)
+            total = acc[span(r), cols] + jnp.dot(
+                held[2, span(r), :], weight[block(far_sib), cols], preferred_element_type=F32
+            )
+            out[span(r), cols] = total.astype(BF16)
+            return 0
+
+        lax.fori_loop(0, tiles, last, 0)
+
+    for r in range(count):
+        far_copies[r].wait_recv()
+        fwd_copies[r].start()
+
+        def middle(j, _, r=r):
+            cols = lanes(j * 256, 256)
+            acc[span(r), cols] += jnp.dot(
+                held[1, span(r), :], weight[block(far), cols], preferred_element_type=F32
+            )
+            return 0
+
+        lax.fori_loop(0, tiles, middle, 0)
+        if r > 0:
+            finish(r - 1)
+    finish(count - 1)
+    for r in range(count):
+        far_copies[r].wait_send()
+        sib_copies[r].wait_send()
+        fwd_copies[r].wait_send()
+
+
+def gather_project(tokens, tangent_tokens, w_inner, w_bmat, w_cmat):
+    length, feat = tokens.shape
+    depth = w_inner.shape[0]
+    total = w_inner.shape[1] + 2 * w_bmat.shape[1]
+    count = 2 * length // SPAN
+    vmem = pl.BlockSpec(memory_space=pltpu.VMEM)
+    anywhere = pl.BlockSpec(memory_space=pl.ANY)
+    dma = pltpu.SemaphoreType.DMA
+    return pl.pallas_call(
+        gather_project_kernel,
+        out_shape=jax.ShapeDtypeStruct((2 * length, total), BF16),
+        in_specs=[vmem, vmem, anywhere, anywhere, anywhere],
+        out_specs=vmem,
+        scratch_shapes=[
+            pltpu.VMEM((3, 2 * length, feat), BF16),
+            pltpu.VMEM((2 * length, total), F32),
+            pltpu.VMEM((depth, total), BF16),
+            dma((3,)),
+        ]
+        + [dma((count,))] * 6,
+        compiler_params=pltpu.CompilerParams(
+            collective_id=0, has_side_effects=True, vmem_limit_bytes=VMEM_LIMIT
+        ),
+        name="gather_project",
+    )(tokens, tangent_tokens, w_inner, w_bmat, w_cmat)
+
+
+def project_scatter_kernel(
+    inner, w_out, out, out_dot,
+    w_far, w_near, p_far, p_near, r_far, s_far, r_x, r_near,
+    w_sem, a_send, a_recv, x_send, x_recv, b_send, b_recv,
+):
+    me = lax.axis_index("head")
+    core = lax.rem(me, 2)
+    chip = (me - core) // 2
+    sib = me + 1 - 2 * core
+    far = lax.rem(me + 2, 4)
+    rows = inner.shape[0]
+    half = w_far.shape[1]
+    feat = half // 2
+    count = rows // SPAN
+    per = count // 2
+    load_far = pltpu.make_async_copy(w_out.at[:, lanes((1 - chip) * half, half)], w_far, w_sem.at[0])
+    load_near = pltpu.make_async_copy(w_out.at[:, lanes(chip * half, half)], w_near, w_sem.at[1])
+    load_far.start()
+    load_near.start()
+    greet([{"head": sib}, {"head": far}])
+    keep = lanes(core * feat, feat)
+    give = lanes((1 - core) * feat, feat)
+    tiles = half // 256
+
+    def multiply(r, weight, into):
+        def one(j, _):
+            cols = lanes(j * 256, 256)
+            into[r, :, cols] = jnp.dot(
+                inner[r * SPAN : (r + 1) * SPAN, :], weight[:, cols], preferred_element_type=F32
+            ).astype(BF16)
+            return 0
+
+        lax.fori_loop(0, tiles, one, 0)
+
+    a_copies = [
+        remote(p_far.at[r, :, give], r_far.at[r], a_send.at[r], a_recv.at[r], {"head": sib})
+        for r in range(count)
+    ]
+    x_copies = [
+        remote(s_far.at[r], r_x.at[r], x_send.at[r], x_recv.at[r], {"head": far})
+        for r in range(count)
+    ]
+    b_copies = [
+        remote(p_near.at[r, :, give], r_near.at[r], b_send.at[r], b_recv.at[r], {"head": sib})
+        for r in range(count)
+    ]
+
+    def pass_on(r):
+        a_copies[r].wait_recv()
+        s_far[r] = (p_far[r, :, keep].astype(F32) + r_far[r].astype(F32)).astype(BF16)
+        x_copies[r].start()
+
+    load_far.wait()
+    for r in range(count):
+        multiply(r, w_far, p_far)
+        a_copies[r].start()
+        if r > 0:
+            pass_on(r - 1)
+    load_near.wait()
+    for r in range(count):
+        multiply(r, w_near, p_near)
+        b_copies[r].start()
+        if r == 0:
+            pass_on(count - 1)
+    for r in range(count):
+        b_copies[r].wait_recv()
+        x_copies[r].wait_recv()
+        total = p_near[r, :, keep].astype(F32) + r_near[r].astype(F32) + r_x[r].astype(F32)
+        ref, at = (out, r) if r < per else (out_dot, r - per)
+        ref[at * SPAN : (at + 1) * SPAN, :] = total.astype(BF16)
+    for r in range(count):
+        a_copies[r].wait_send()
+        b_copies[r].wait_send()
+        x_copies[r].wait_send()
+
+
+def project_scatter(inner, w_out):
+    rows, width = inner.shape
+    full = w_out.shape[1]
+    half, feat = full // 2, full // 4
+    count = rows // SPAN
+    vmem = pl.BlockSpec(memory_space=pltpu.VMEM)
+    dma = pltpu.SemaphoreType.DMA
+    result = jax.ShapeDtypeStruct((rows // 2, feat), BF16)
+    return pl.pallas_call(
+        project_scatter_kernel,
+        out_shape=(result, result),
+        in_specs=[vmem, pl.BlockSpec(memory_space=pl.ANY)],
+        out_specs=(vmem, vmem),
+        scratch_shapes=[
+            pltpu.VMEM((width, half), BF16),
+            pltpu.VMEM((width, half), BF16),
+            pltpu.VMEM((count, SPAN, half), BF16),
+            pltpu.VMEM((count, SPAN, half), BF16),
+        ]
+        + [pltpu.VMEM((count, SPAN, feat), BF16)] * 4
+        + [dma((2,))]
+        + [dma((count,))] * 6,
+        compiler_params=pltpu.CompilerParams(
+            collective_id=2, has_side_effects=True, vmem_limit_bytes=VMEM_LIMIT
+        ),
+        name="project_scatter",
+    )(inner, w_out)
+
+
+def mix_kernel(
+    proj, decay, decay_dot, conv_in, conv_bc, skip, out,
+    halo, padded, pad_dec, cum, cum_dot, cum_t, cum_dot_t, wide, wide_dot, x, x_dot, bc, bc_dot,
+    score, score_dot, within, within_dot, state, state_dot,
+    total, rows, pair_total, pair_rows, chain_in, chain_out, give, entry,
+    halo_send, halo_recv, pair_send, pair_recv, chain_send, chain_recv, give_send, give_recv,
+):
+    me = lax.axis_index("ctx")
+    count = lax.axis_size("ctx")
+    odd = lax.rem(me, 2)
+    partner = me + 1 - 2 * odd
+    length = proj.shape[0] // 2
+    width = x.shape[1]
+    heads = decay.shape[1]
+    pairs = width // 128
+    half = pairs // 2
+    blocks = length // SPAN
+    state_len = bc.shape[1] // 2
+    lane = lax.broadcasted_iota(jnp.int32, (1, 128), 1)
+
+    barrier = pltpu.get_barrier_semaphore()
+    for step in (-2, -1, 1, 2):
+        other = me + step
+
+        @pl.when(jnp.logical_and(other >= 0, other < count))
+        def _(other=other):
+            pl.semaphore_signal(barrier, inc=1, device_id={"ctx": other}, device_id_type=MESH)
+
+    pl.semaphore_wait(barrier, jnp.minimum(me, 2) + jnp.minimum(count - 1 - me, 2))
+
+    halo_copies = [
+        remote(
+            proj.at[(k + 1) * length - 16 : (k + 1) * length, :],
+            halo.at[k],
+            halo_send.at[k],
+            halo_recv.at[k],
+            {"ctx": me + 1},
+        )
+        for k in range(2)
+    ]
+
+    @pl.when(me + 1 < count)
+    def _():
+        for copy in halo_copies:
+            copy.start()
+
+    @pl.when(me < 2)
+    def _():
+        chain_in[...] = jnp.zeros_like(chain_in)
+
+    pad_dec[...] = jnp.zeros_like(pad_dec)
+    pad_dec[0, :, 0:heads] = decay[...]
+    pad_dec[1, :, 0:heads] = decay_dot[...]
+    t_index = lax.broadcasted_iota(jnp.int32, (SPAN, SPAN), 0)
+    s_index = lax.broadcasted_iota(jnp.int32, (SPAN, SPAN), 1)
+    lower = (t_index >= s_index).astype(F32)
+    for b in range(blocks):
+        at = slice(b * SPAN, (b + 1) * SPAN)
+        for source, into, into_t in ((0, cum, cum_t), (1, cum_dot, cum_dot_t)):
+            summed = jnp.dot(lower, pad_dec[source, at, :], precision=HIGHEST, preferred_element_type=F32)
+            into[at, :] = summed
+            into_t[b] = summed.T
+    cum[length : length + 8, :] = jnp.zeros((8, 128), F32)
+    cum[length : length + 1, 0:heads] = skip[...]
+
+    def expand(p, _):
+        cols = lanes(p * 128, 128)
+        source = lax.broadcasted_iota(jnp.int32, (128, 128), 0)
+        target = lax.broadcasted_iota(jnp.int32, (128, 128), 1)
+        pick = (source == 2 * p + (target >= HEAD_DIM).astype(jnp.int32)).astype(F32)
+        wide[:, cols] = jnp.dot(cum[...], pick, precision=HIGHEST, preferred_element_type=F32)
+        wide_dot[:, cols] = jnp.dot(cum_dot[...], pick, precision=HIGHEST, preferred_element_type=F32)
+        return 0
+
+    lax.fori_loop(0, pairs, expand, 0)
+
+    @pl.when(me == 0)
+    def _():
+        halo[...] = jnp.zeros_like(halo)
+
+    @pl.when(me > 0)
+    def _():
+        for copy in halo_copies:
+            copy.wait_recv()
+
+    def convolve(cols, kernel, into, into_dot, to):
+        for b in range(blocks):
+            start = b * SPAN
+            convs = []
+            for k in range(2):
+                if b == 0:
+                    padded[k, 0:16, :] = halo[k, :, cols].astype(F32)
+                else:
+                    padded[k, 0:16, :] = proj[k * length + start - 16 : k * length + start, cols].astype(F32)
+                padded[k, 16 : 16 + SPAN, :] = proj[k * length + start : k * length + start + SPAN, cols].astype(F32)
+                summed = kernel[0:1, :] * padded[k, 13 : 13 + SPAN, :]
+                for tap in range(1, 4):
+                    summed = summed + kernel[tap : tap + 1, :] * padded[k, 13 + tap : 13 + tap + SPAN, :]
+                convs.append(summed)
+            gate = 1.0 / (1.0 + jnp.exp(-convs[0]))
+            into[start : start + SPAN, to] = (convs[0] * gate).astype(BF16)
+            into_dot[start : start + SPAN, to] = (
+                convs[1] * (gate * (1.0 + convs[0] * (1.0 - gate)))
+            ).astype(BF16)
+
+    for k in range(2):
+        span = slice(k * state_len, (k + 1) * state_len)
+        convolve(
+            slice(width + k * state_len, width + (k + 1) * state_len), conv_bc[:, span], bc, bc_dot, span
+        )
+
+    def convolve_inner(p, _):
+        cols = lanes(p * 128, 128)
+        convolve(cols, conv_in[:, cols], x, x_dot, cols)
+        return 0
+
+    lax.fori_loop(0, pairs, convolve_inner, 0)
+
+    writer_t = [bc[b * SPAN : (b + 1) * SPAN, 0:state_len].T for b in range(blocks)]
+    writer_dot_t = [bc_dot[b * SPAN : (b + 1) * SPAN, 0:state_len].T for b in range(blocks)]
+
+    def states(p, _):
+        cols = lanes(p * 128, 128)
+        sums = None
+        for b in range(blocks):
+            at = slice(b * SPAN, (b + 1) * SPAN)
+            end = slice((b + 1) * SPAN - 1, (b + 1) * SPAN)
+            last, last_dot = wide[end, cols], wide_dot[end, cols]
+            remaining = jnp.exp(last - wide[at, cols])
+            values = x[at, cols].astype(F32)
+            scaled = (values * remaining).astype(BF16)
+            scaled_dot = (
+                (x_dot[at, cols].astype(F32) + values * (last_dot - wide_dot[at, cols])) * remaining
+            ).astype(BF16)
+            new = jnp.dot(writer_t[b], scaled, preferred_element_type=F32)
+            new_dot = jnp.dot(writer_t[b], scaled_dot, preferred_element_type=F32) + jnp.dot(
+                writer_dot_t[b], scaled, preferred_element_type=F32
+            )
+            state[b, :, cols] = new
+            state_dot[b, :, cols] = new_dot
+            if sums is None:
+                sums = (last, last_dot, new, new_dot)
+            else:
+                log, slope, old, old_dot = sums
+                retain = jnp.exp(last)
+                sums = (
+                    log + last,
+                    slope + last_dot,
+                    retain * old + new,
+                    retain * (old_dot + last_dot * old) + new_dot,
+                )
+        log, slope, old, old_dot = sums
+        rows[p] = jnp.concatenate([log, slope, jnp.zeros((6, 128), F32)], 0)
+        total[p, 0] = old.astype(BF16)
+        total[p, 1] = old_dot.astype(BF16)
+        return 0
+
+    lax.fori_loop(0, pairs, states, 0)
+
+    mine = odd * half
+    others = (1 - odd) * half
+    pair_copies = [
+        remote(total.at[pl.ds(others, half)], pair_total, pair_send.at[0], pair_recv.at[0], {"ctx": partner}),
+        remote(rows.at[pl.ds(others, half)], pair_rows, pair_send.at[1], pair_recv.at[1], {"ctx": partner}),
+    ]
+    for copy in pair_copies:
+        copy.start()
+
+    def outer_t(left, right):
+        return lax.dot_general(left, right, (((1,), (1,)), ((), ())), preferred_element_type=F32)
+
+    for b in range(blocks):
+        at = slice(b * SPAN, (b + 1) * SPAN)
+        writer, reader = bc[at, 0:state_len], bc[at, state_len : 2 * state_len]
+        writer_dot, reader_dot = bc_dot[at, 0:state_len], bc_dot[at, state_len : 2 * state_len]
+        causal = t_index >= s_index
+        score[b] = jnp.where(causal, outer_t(reader, writer), 0.0)
+        score_dot[b] = jnp.where(causal, outer_t(reader_dot, writer) + outer_t(reader, writer_dot), 0.0)
+
+    def mixing(p, _):
+        cols = lanes(p * 128, 128)
+        for b in range(blocks):
+            for t in range(SPAN // 128):
+                size = (t + 1) * 128
+                at = slice(b * SPAN + t * 128, b * SPAN + size)
+                upto = slice(b * SPAN, b * SPAN + size)
+                tile = slice(t * 128, size)
+                values = x[upto, cols]
+                both = jnp.concatenate([values, x_dot[upto, cols]], 1)
+                column, column_dot = wide[at, cols], wide_dot[at, cols]
+                found = []
+                for k in range(2):
+                    first = k * HEAD_DIM
+                    row = cum_t[b, pl.ds(2 * p + k, 1), :][:, 0:size]
+                    row_dot = cum_dot_t[b, pl.ds(2 * p + k, 1), :][:, 0:size]
+                    weight = jnp.exp(jnp.minimum(column[:, first : first + 1] - row, 0.0))
+                    change = column_dot[:, first : first + 1] - row_dot
+                    scores = score[b, tile, 0:size]
+                    mix = (weight * scores).astype(BF16)
+                    mix_dot = (weight * (score_dot[b, tile, 0:size] + change * scores)).astype(BF16)
+                    found.append(
+                        (
+                            jnp.dot(mix, both, preferred_element_type=F32),
+                            jnp.dot(mix_dot, values, preferred_element_type=F32),
+                        )
+                    )
+                (r0, q0), (r1, q1) = found
+                within[at, cols] = jnp.where(lane < HEAD_DIM, r0[:, 0:128], r1[:, 0:128])
+                within_dot[at, cols] = jnp.where(lane < HEAD_DIM, r0[:, 128:256] + q0, r1[:, 128:256] + q1)
+        return 0
+
+    lax.fori_loop(0, pairs, mixing, 0)
+
+    for copy in pair_copies:
+        copy.wait_recv()
+
+    chain_copies = [
+        remote(chain_out.at[i], chain_in.at[i], chain_send.at[i], chain_recv.at[i], {"ctx": me + 2})
+        for i in range(half)
+    ]
+    give_copies = [
+        remote(give.at[i], entry.at[mine + i], give_send.at[i], give_recv.at[i], {"ctx": partner})
+        for i in range(half)
+    ]
+    first_here = odd == 0
+    for i in range(half):
+
+        @pl.when(me >= 2)
+        def _(i=i):
+            chain_copies[i].wait_recv()
+
+        arrived, arrived_dot = chain_in[i, 0].astype(F32), chain_in[i, 1].astype(F32)
+        own, own_dot = total[mine + i, 0].astype(F32), total[mine + i, 1].astype(F32)
+        their, their_dot = pair_total[i, 0].astype(F32), pair_total[i, 1].astype(F32)
+        own_rows, their_rows = rows[mine + i], pair_rows[i]
+        early_rows = jnp.where(first_here, own_rows, their_rows)
+        late_rows = jnp.where(first_here, their_rows, own_rows)
+        retain = jnp.exp(early_rows[0:1])
+        middle = retain * arrived + jnp.where(first_here, own, their)
+        middle_dot = retain * (arrived_dot + early_rows[1:2] * arrived) + jnp.where(
+            first_here, own_dot, their_dot
+        )
+        retain = jnp.exp(late_rows[0:1])
+        chain_out[i, 0] = (retain * middle + jnp.where(first_here, their, own)).astype(BF16)
+        chain_out[i, 1] = (
+            retain * (middle_dot + late_rows[1:2] * middle) + jnp.where(first_here, their_dot, own_dot)
+        ).astype(BF16)
+
+        @pl.when(me + 2 < count)
+        def _(i=i):
+            chain_copies[i].start()
+
+        give[i, 0] = jnp.where(first_here, middle, arrived).astype(BF16)
+        give[i, 1] = jnp.where(first_here, middle_dot, arrived_dot).astype(BF16)
+        give_copies[i].start()
+        entry[mine + i, 0] = jnp.where(first_here, arrived, middle).astype(BF16)
+        entry[mine + i, 1] = jnp.where(first_here, arrived_dot, middle_dot).astype(BF16)
+
+    def finish(p, _):
+        cols = lanes(p * 128, 128)
+        gain = wide[length : length + 1, cols]
+        now, now_dot = entry[p, 0], entry[p, 1]
+        for b in range(blocks):
+            at = slice(b * SPAN, (b + 1) * SPAN)
+            end = slice((b + 1) * SPAN - 1, (b + 1) * SPAN)
+            reader = bc[at, state_len : 2 * state_len]
+            reader_dot = bc_dot[at, state_len : 2 * state_len]
+            read = jnp.dot(reader, jnp.concatenate([now, now_dot], 1), preferred_element_type=F32)
+            moved = jnp.dot(reader_dot, now, preferred_element_type=F32)
+            grown = jnp.exp(wide[at, cols])
+            plain = read[:, 0:128]
+            out[at, cols] = (
+                within[at, cols] + grown * plain + gain * x[at, cols].astype(F32)
+            ).astype(BF16)
+            out[length + b * SPAN : length + (b + 1) * SPAN, cols] = (
+                within_dot[at, cols]
+                + grown * (read[:, 128:256] + moved + wide_dot[at, cols] * plain)
+                + gain * x_dot[at, cols].astype(F32)
+            ).astype(BF16)
+            if b + 1 < blocks:
+                retain = jnp.exp(wide[end, cols])
+                old, old_dot = now.astype(F32), now_dot.astype(F32)
+                now = (retain * old + state[b, :, cols]).astype(BF16)
+                now_dot = (
+                    retain * (old_dot + wide_dot[end, cols] * old) + state_dot[b, :, cols]
+                ).astype(BF16)
+        return 0
+
+    lax.fori_loop(mine, mine + half, finish, 0)
+    back_copies = [
+        remote(give.at[i], entry.at[others + i], give_send.at[i], give_recv.at[i], {"ctx": partner})
+        for i in range(half)
+    ]
+    for i in range(half):
+        back_copies[i].wait_recv()
+    lax.fori_loop(others, others + half, finish, 0)
+
+    for copy in pair_copies + give_copies:
+        copy.wait_send()
+
+    @pl.when(me + 1 < count)
+    def _():
+        for copy in halo_copies:
+            copy.wait_send()
+
+    @pl.when(me + 2 < count)
+    def _():
+        for copy in chain_copies:
+            copy.wait_send()
+
+
+def mix(projected, log_decay, tangent_decay, conv_inner, conv_bc, skip_gain):
+    length = log_decay.shape[0]
+    width = conv_inner.shape[1]
+    state_len = conv_bc.shape[1] // 2
+    blocks = length // SPAN
+    pairs = width // 128
+    half = pairs // 2
+    vmem = pl.BlockSpec(memory_space=pltpu.VMEM)
+    dma = pltpu.SemaphoreType.DMA
+    piece = (2, state_len, 128)
+    return pl.pallas_call(
+        mix_kernel,
+        out_shape=jax.ShapeDtypeStruct((2 * length, width), BF16),
+        in_specs=[vmem] * 6,
+        out_specs=vmem,
+        scratch_shapes=[
+            pltpu.VMEM((2, 16, width + 2 * state_len), BF16),
+            pltpu.VMEM((2, 16 + SPAN, 128), F32),
+            pltpu.VMEM((2, length, 128), F32),
+            pltpu.VMEM((length + 8, 128), F32),
+            pltpu.VMEM((length, 128), F32),
+            pltpu.VMEM((blocks, 128, SPAN), F32),
+            pltpu.VMEM((blocks, 128, SPAN), F32),
+            pltpu.VMEM((length + 8, width), F32),
+            pltpu.VMEM((length, width), F32),
+            pltpu.VMEM((length, width), BF16),
+            pltpu.VMEM((length, width), BF16),
+            pltpu.VMEM((length, 2 * state_len), BF16),
+            pltpu.VMEM((length, 2 * state_len), BF16),
+            pltpu.VMEM((blocks, SPAN, SPAN), F32),
+            pltpu.VMEM((blocks, SPAN, SPAN), F32),
+            pltpu.VMEM((length, width), F32),
+            pltpu.VMEM((length, width), F32),
+            pltpu.VMEM((blocks, state_len, width), F32),
+            pltpu.VMEM((blocks, state_len, width), F32),
+            pltpu.VMEM((pairs, *piece), BF16),
+            pltpu.VMEM((pairs, 8, 128), F32),
+            pltpu.VMEM((half, *piece), BF16),
+            pltpu.VMEM((half, 8, 128), F32),
+            pltpu.VMEM((half, *piece), BF16),
+            pltpu.VMEM((half, *piece), BF16),
+            pltpu.VMEM((half, *piece), BF16),
+            pltpu.VMEM((pairs, *piece), BF16),
+            dma((2,)),
+            dma((2,)),
+            dma((2,)),
+            dma((2,)),
+            dma((half,)),
+            dma((half,)),
+            dma((half,)),
+            dma((half,)),
+        ],
+        compiler_params=pltpu.CompilerParams(
+            collective_id=1, has_side_effects=True, vmem_limit_bytes=VMEM_LIMIT
+        ),
+        name="mix",
+    )(projected, log_decay, tangent_decay, conv_inner, conv_bc, skip_gain.reshape(1, -1))
+
+
+def fused_on_device(
+    tokens, tangent_tokens, log_decay, tangent_decay, w_inner, w_bmat, w_cmat,
+    conv_inner, conv_bc, skip_gain, w_out,
+):
+    projected = gather_project(tokens, tangent_tokens, w_inner, w_bmat, w_cmat)
+    inner = mix(projected, log_decay, tangent_decay, conv_inner, conv_bc, skip_gain)
+    return project_scatter(inner, w_out)
 
 
 def shifted(block, axis, distance):
@@ -188,6 +823,7 @@
         P("head", None),
     )
     out_specs = (P("ctx", "head"), P("ctx", "head"))
+    fits = mesh.shape["head"] == 4 and mesh.shape["ctx"] % 2 == 0
     return jax.shard_map(
-        on_device, mesh=mesh, in_specs=in_specs, out_specs=out_specs, check_vma=False
-    )
+        fused_on_device if fits else on_device, mesh=mesh, in_specs=in_specs, out_specs=out_specs, check_vma=False
+    )

time: 377 us -> 133 us (0.35)
  waiting for transfers between devices: 188 us -> 0 us
  Pallas kernels: 0 us -> 124 us
  local copies, waits for them, and re-layouts: 54.8 us -> 7.24 us
  matrix products: 44.1 us -> 0 us
  other arithmetic: 35.5 us -> 0 us
  blocking collectives: 35 us -> 0 us
  between operations: 14.5 us -> 0.65 us
    all_gather x3 -> x0, waiting for transfers between devices: 131 us -> none  [the longest x2 96.9 us: carried_in(): gathered = jax.tree.map(lambda a: lax.all_gather(a, axis), part)]
    pallas_call x0 -> x3, Pallas kernels: none -> 124 us  [the longest x1 47.7 us: mix(): pl.pallas_call(mix_kernel, out_shape=jax.ShapeDtypeStruct((2 * length, wi...]
    unnamed x5 -> x0, waiting for transfers between devices: 53.2 us -> none
    dot_general x19 -> x0, matrix products: 44.1 us -> none  [the longest x3 12.7 us: span_parts(): jnp.einsum('hts,shp->thp', mixing, inputs, preferred_element_type=jnp.flo...]
    all_gather x2 -> x0, blocking collectives: 35 us -> none  [carried_in(): gathered = jax.tree.map(lambda a: lax.all_gather(a, axis), part)]
    add x9 -> x0, other arithmetic: 14.7 us -> none  [the longest x7 12.8 us: combine(): retain * (early_tangent + late_slope * early_state) + late_tangent]
    slice x15 -> x0, local copies, waits for them, and re-layouts: 12.8 us -> none  [the longest x4 7.29 us: separate(): inputs = values[:, :width].reshape(blocks, SPAN, heads_here, HEAD_DIM)]
    convert_element_type x4 -> x0, local copies, waits for them, and re-layouts: 11.4 us -> none  [finish(): skip_gain[None, :, None] * inputs[position]]
  transfers between devices with their start and end apart: 5 -> 0, of which waited for: 5 -> 0; matrix products, arithmetic and copies ran while one was open for 12% -> 0% of each run, Pallas kernels for 0% -> 0%
where the time goes in v1:
time: 133 us; the launch traced here: 132 us
  Pallas kernels  124 us (93%)
  local copies, waits for them, and re-layouts  7.24 us (5%)
    pallas_call x1, Pallas kernels, mix(): pl.pallas_call(mix_kernel, out_shape=jax.ShapeDtypeStruct((2 * length, wi...  47.7 us
    pallas_call x1, Pallas kernels, gather_project(): pl.pallas_call(gather_project_kernel, out_shape=jax.ShapeDtypeStruct((2 *...  39.1 us
    pallas_call x1, Pallas kernels, project_scatter(): pl.pallas_call(project_scatter_kernel, out_shape=(result, result), in_spe...  37.6 us
    unnamed x4, local copies, waits for them, and re-layouts  7.24 us

profile of v1, /device:TPU:28, one launch (start us, length us, event | category | flops | bytes accessed | tf_op | source)
XLA Modules:
  0.0 132.2 jit_solution(15492689800536363830)
XLA Ops:
  0.6 1.6 %copy.13.decay = f32[512,20]{1,0:T(8,128)} copy(f32[512,20]{0,1:T(8,128)} %param.13) | data formatting | bytes 81920 | tf_op args[2]
  2.3 1.6 %copy.14.decay_dot = f32[512,20]{1,0:T(8,128)} copy(f32[512,20]{0,1:T(8,128)} %param.14) | data formatting | bytes 81920 | tf_op args[3]
  3.9 39.1 %gather_project.1.proj = bf16[1024,1536]{1,0:T(8,128)(2,1)} custom-call(bf16[512,640]{1,0:T(8,128)(2,1)} %tok.1, bf16[512,640]{1,0:T(8,128)(2,1)} %tan.1, bf16[2560,1280]{1,0:T(8,128)(2,1)} %w_in.1, bf16[2560,128]{1,0:T(8,128)(2,1)} %w_b.1, bf16[2560,128]{1,0:T(8,128)(2,1)} %w_c.1), custom_call_target="tpu_custom_call" | custom-call | tf_op jit(solution)/shard_map/gather_project/pallas_call | solution.py:142
  43.0 47.7 %mix.1.inner = bf16[1024,1280]{1,0:T(8,128)(2,1)} custom-call(bf16[1024,1536]{1,0:T(8,128)(2,1)} %gather_project.1.proj, f32[512,20]{1,0:T(8,128)} %copy.13.decay, f32[512,20]{1,0:T(8,128)} %copy.14.decay_dot, f32[4,1280]{1,0:T(4,128)} %conv_in.1, f32[4,256]{1,0:T(4,128)} %conv_bc.1, f32[1,20]{1,0:T(1,128)} %bitcast.1), custom_call_target="tpu_custom_call" | custom-call | tf_op jit(solution)/shard_map/mix/pallas_call | solution.py:587
  90.7 37.6 %project_scatter.1 = (bf16[512,640]{1,0:T(8,128)(2,1)}, bf16[512,640]{1,0:T(8,128)(2,1)}) custom-call(bf16[1024,1280]{1,0:T(8,128)(2,1)} %mix.1.inner, bf16[1280,2560]{1,0:T(8,128)(2,1)} %w_out.1), custom_call_target="tpu_custom_call" | custom-call | tf_op jit(solution)/shard_map/project_scatter/pallas_call | solution.py:245
  128.3 2.0 %copy.17 = bf16[512,640]{1,0:T(8,128)(2,1)} copy(bf16[512,640]{1,0:T(8,128)(2,1)} %get-tuple-element.4) | data formatting | bytes 1310720
  130.3 2.0 %copy.18 = bf16[512,640]{1,0:T(8,128)(2,1)} copy(bf16[512,640]{1,0:T(8,128)(2,1)} %get-tuple-element.5) | data formatting | bytes 1310720

commit v2 on v0

--- a/solution.py
+++ b/solution.py
@@ -1,10 +1,590 @@
+import functools
+
 import jax
 import jax.numpy as jnp
 from jax import lax
+from jax.experimental import pallas as pl
+from jax.experimental.pallas import tpu as pltpu
 from jax.sharding import PartitionSpec as P
 
 HEAD_DIM = 64
 SPAN = 256
+MESH = pl.DeviceIdType.MESH
+HIGHEST = lax.Precision.HIGHEST
+VMEM_LIMIT = 60 * 1024 * 1024
+F32 = jnp.float32
+BF16 = jnp.bfloat16
+
+
+def remote(src, dst, send, recv, device):
+    return pltpu.make_async_remote_copy(
+        src_ref=src, dst_ref=dst, send_sem=send, recv_sem=recv, device_id=device, device_id_type=MESH
+    )
+
+
+def lanes(start, size):
+    return pl.ds(pl.multiple_of(start, 128), size)
+
+
+def layer_kernel(
+    tok, tan, decay_t, decay_dot_t, w_in, w_b, w_c, conv_in, conv_bc, skip, w_out, out, out_dot,
+    held, acc, weight, proj, inner,
+    halo, padded, pad_dec, cum, cum_dot, cum_t, cum_dot_t, wide, wide_dot, x, x_dot, bc, bc_dot,
+    score, score_dot, within, within_dot, state, state_dot,
+    total, rows, pair_total, pair_rows, chain_in, chain_out, give, entry,
+    p_near, r_far, s_far, r_x, r_near,
+    w_sem, sib_send, sib_recv, far_send, far_recv, fwd_send, fwd_recv,
+    halo_send, halo_recv, pair_send, pair_recv, chain_send, chain_recv, give_send, give_recv,
+    a_send, a_recv, x_send, x_recv, b_send, b_recv,
+):
+    head = lax.axis_index("head")
+    core = lax.rem(head, 2)
+    chip = (head - core) // 2
+    sib = head + 1 - 2 * core
+    far = lax.rem(head + 2, 4)
+    far_sib = lax.rem(sib + 2, 4)
+    me = lax.axis_index("ctx")
+    count = lax.axis_size("ctx")
+    odd = lax.rem(me, 2)
+    partner = me + 1 - 2 * odd
+    length, feat = tok.shape
+    width = x.shape[1]
+    heads = decay_t.shape[0]
+    pairs = width // 128
+    half = pairs // 2
+    blocks = length // SPAN
+    state_len = bc.shape[1] // 2
+    lane = lax.broadcasted_iota(jnp.int32, (1, 128), 1)
+
+    loads = [
+        pltpu.make_async_copy(w_in, weight.at[:, 0:width], w_sem.at[0]),
+        pltpu.make_async_copy(w_b, weight.at[:, width : width + state_len], w_sem.at[1]),
+        pltpu.make_async_copy(w_c, weight.at[:, width + state_len :], w_sem.at[2]),
+    ]
+    for load in loads:
+        load.start()
+
+    barrier = pltpu.get_barrier_semaphore()
+    for other in (sib, far):
+        pl.semaphore_signal(barrier, inc=1, device_id={"head": other}, device_id_type=MESH)
+    for step in (-2, -1, 1, 2):
+        other = me + step
+
+        @pl.when(jnp.logical_and(other >= 0, other < count))
+        def _(other=other):
+            pl.semaphore_signal(barrier, inc=1, device_id={"ctx": other}, device_id_type=MESH)
+
+    pl.semaphore_wait(barrier, 2 + jnp.minimum(me, 2) + jnp.minimum(count - 1 - me, 2))
+
+    cut = length - SPAN - 16
+    chunks = [(0, cut, length - cut), (1, cut, length - cut), (0, 0, cut), (1, 0, cut)]
+
+    def own(c):
+        k, start, size = chunks[c]
+        return (tok, tan)[k].at[start : start + size]
+
+    def span(c):
+        k, start, size = chunks[c]
+        return slice(k * length + start, k * length + start + size)
+
+    order = range(len(chunks))
+    far_copies = [
+        remote(own(c), held.at[1, span(c)], far_send.at[c], far_recv.at[c], {"head": far}) for c in order
+    ]
+    sib_copies = [
+        remote(own(c), held.at[0, span(c)], sib_send.at[c], sib_recv.at[c], {"head": sib}) for c in order
+    ]
+    fwd_copies = [
+        remote(held.at[1, span(c)], held.at[2, span(c)], fwd_send.at[c], fwd_recv.at[c], {"head": sib})
+        for c in order
+    ]
+    for c in order:
+        far_copies[c].start()
+        sib_copies[c].start()
+    tiles = weight.shape[1] // 256
+
+    def block(index):
+        return pl.ds(pl.multiple_of(index * feat, 128), feat)
+
+    def near(c):
+        sib_copies[c].wait_recv()
+        size = chunks[c][2]
+
+        def one(j, _):
+            cols = lanes(j * 256, 256)
+            acc[0:size, cols] = jnp.dot(
+                own(c)[...], weight[block(head), cols], preferred_element_type=F32
+            ) + jnp.dot(held[0, span(c), :], weight[block(sib), cols], preferred_element_type=F32)
+            return 0
+
+        lax.fori_loop(0, tiles, one, 0)
+
+    def forward(c):
+        far_copies[c].wait_recv()
+        fwd_copies[c].start()
+
+    def distant(c):
+        size = chunks[c][2]
+
+        def middle(j, _):
+            cols = lanes(j * 256, 256)
+            acc[0:size, cols] += jnp.dot(
+                held[1, span(c), :], weight[block(far), cols], preferred_element_type=F32
+            )
+            return 0
+
+        lax.fori_loop(0, tiles, middle, 0)
+        fwd_copies[c].wait_recv()
+
+        def last(j, _):
+            cols = lanes(j * 256, 256)
+            summed = acc[0:size, cols] + jnp.dot(
+                held[2, span(c), :], weight[block(far_sib), cols], preferred_element_type=F32
+            )
+            proj[span(c), cols] = summed.astype(BF16)
+            return 0
+
+        lax.fori_loop(0, tiles, last, 0)
+
+    @pl.when(me < 2)
+    def _():
+        chain_in[...] = jnp.zeros_like(chain_in)
+
+    @pl.when(me == 0)
+    def _():
+        halo[...] = jnp.zeros_like(halo)
+
+    pad_dec[...] = jnp.zeros_like(pad_dec)
+    pad_dec[0, 0:heads, :] = decay_t[...]
+    pad_dec[1, 0:heads, :] = decay_dot_t[...]
+    t_index = lax.broadcasted_iota(jnp.int32, (SPAN, SPAN), 0)
+    s_index = lax.broadcasted_iota(jnp.int32, (SPAN, SPAN), 1)
+    upper = (t_index <= s_index).astype(F32)
+    for b in range(blocks):
+        at = slice(b * SPAN, (b + 1) * SPAN)
+        for source, into, into_t in ((0, cum, cum_t), (1, cum_dot, cum_dot_t)):
+            summed = jnp.dot(pad_dec[source, :, at], upper, precision=HIGHEST, preferred_element_type=F32)
+            into_t[b] = summed
+            into[at, :] = summed.T
+    cum[length : length + 8, :] = jnp.zeros((8, 128), F32)
+    cum[length : length + 1, 0:heads] = skip[...]
+
+    def expand(p, _):
+        cols = lanes(p * 128, 128)
+        source = lax.broadcasted_iota(jnp.int32, (128, 128), 0)
+        target = lax.broadcasted_iota(jnp.int32, (128, 128), 1)
+        pick = (source == 2 * p + (target >= HEAD_DIM).astype(jnp.int32)).astype(F32)
+        wide[:, cols] = jnp.dot(cum[...], pick, precision=HIGHEST, preferred_element_type=F32)
+        wide_dot[:, cols] = jnp.dot(cum_dot[...], pick, precision=HIGHEST, preferred_element_type=F32)
+        return 0
+
+    lax.fori_loop(0, pairs, expand, 0)
+
+    def convolve(b, cols, kernel, into, into_dot, to):
+        start = b * SPAN
+        convs = []
+        for k in range(2):
+            if b == 0:
+                padded[k, 0:16, :] = halo[k, :, cols].astype(F32)
+            else:
+                padded[k, 0:16, :] = proj[k * length + start - 16 : k * length + start, cols].astype(F32)
+            padded[k, 16 : 16 + SPAN, :] = proj[k * length + start : k * length + start + SPAN, cols].astype(F32)
+            summed = kernel[0:1, :] * padded[k, 13 : 13 + SPAN, :]
+            for tap in range(1, 4):
+                summed = summed + kernel[tap : tap + 1, :] * padded[k, 13 + tap : 13 + tap + SPAN, :]
+            convs.append(summed)
+        gate = 1.0 / (1.0 + jnp.exp(-convs[0]))
+        into[start : start + SPAN, to] = (convs[0] * gate).astype(BF16)
+        into_dot[start : start + SPAN, to] = (
+            convs[1] * (gate * (1.0 + convs[0] * (1.0 - gate)))
+        ).astype(BF16)
+
+    def convolve_all(b):
+        for k in range(2):
+            part = slice(k * state_len, (k + 1) * state_len)
+            convolve(
+                b, slice(width + k * state_len, width + (k + 1) * state_len), conv_bc[:, part], bc, bc_dot, part
+            )
+
+        def convolve_inner(p, _):
+            cols = lanes(p * 128, 128)
+            convolve(b, cols, conv_in[:, cols], x, x_dot, cols)
+            return 0
+
+        lax.fori_loop(0, pairs, convolve_inner, 0)
+
+    def states_all(b):
+        at = slice(b * SPAN, (b + 1) * SPAN)
+        end = slice((b + 1) * SPAN - 1, (b + 1) * SPAN)
+        writer_t = bc[at, 0:state_len].T
+        writer_dot_t = bc_dot[at, 0:state_len].T
+
+        def states(p, _):
+            cols = lanes(p * 128, 128)
+            last, last_dot = wide[end, cols], wide_dot[end, cols]
+            remaining = jnp.exp(last - wide[at, cols])
+            values = x[at, cols].astype(F32)
+            scaled = (values * remaining).astype(BF16)
+            scaled_dot = (
+                (x_dot[at, cols].astype(F32) + values * (last_dot - wide_dot[at, cols])) * remaining
+            ).astype(BF16)
+            new = jnp.dot(writer_t, scaled, preferred_element_type=F32)
+            new_dot = jnp.dot(writer_t, scaled_dot, preferred_element_type=F32) + jnp.dot(
+                writer_dot_t, scaled, preferred_element_type=F32
+            )
+            state[b, :, cols] = new
+            state_dot[b, :, cols] = new_dot
+            if b == 0:
+                final = slice(2 * SPAN - 1, 2 * SPAN)
+                log, slope = wide[final, cols], wide_dot[final, cols]
+                retain = jnp.exp(log)
+                rows[p] = jnp.concatenate([last + log, last_dot + slope, jnp.zeros((6, 128), F32)], 0)
+                total[p, 0] = (retain * new + state[1, :, cols]).astype(BF16)
+                total[p, 1] = (retain * (new_dot + slope * new) + state_dot[1, :, cols]).astype(BF16)
+            return 0
+
+        lax.fori_loop(0, pairs, states, 0)
+
+    def outer_t(left, right):
+        return lax.dot_general(left, right, (((1,), (1,)), ((), ())), preferred_element_type=F32)
+
+    def score_all(b):
+        at = slice(b * SPAN, (b + 1) * SPAN)
+        writer, reader = bc[at, 0:state_len], bc[at, state_len : 2 * state_len]
+        writer_dot, reader_dot = bc_dot[at, 0:state_len], bc_dot[at, state_len : 2 * state_len]
+        causal = t_index >= s_index
+        score[b] = jnp.where(causal, outer_t(reader, writer), 0.0)
+        score_dot[b] = jnp.where(causal, outer_t(reader_dot, writer) + outer_t(reader, writer_dot), 0.0)
+
+    def mixing(b, p, _):
+        cols = lanes(p * 128, 128)
+        for t in range(SPAN // 128):
+            size = (t + 1) * 128
+            at = slice(b * SPAN + t * 128, b * SPAN + size)
+            upto = slice(b * SPAN, b * SPAN + size)
+            tile = slice(t * 128, size)
+            values = x[upto, cols]
+            both = jnp.concatenate([values, x_dot[upto, cols]], 1)
+            column, column_dot = wide[at, cols], wide_dot[at, cols]
+            found = []
+            for k in range(2):
+                first = k * HEAD_DIM
+                row = cum_t[b, pl.ds(2 * p + k, 1), :][:, 0:size]
+                row_dot = cum_dot_t[b, pl.ds(2 * p + k, 1), :][:, 0:size]
+                weight = jnp.exp(jnp.minimum(column[:, first : first + 1] - row, 0.0))
+                change = column_dot[:, first : first + 1] - row_dot
+                scores = score[b, tile, 0:size]
+                mix = (weight * scores).astype(BF16)
+                mix_dot = (weight * (score_dot[b, tile, 0:size] + change * scores)).astype(BF16)
+                found.append(
+                    (
+                        jnp.dot(mix, both, preferred_element_type=F32),
+                        jnp.dot(mix_dot, values, preferred_element_type=F32),
+                    )
+                )
+            (r0, q0), (r1, q1) = found
+            within[at, cols] = jnp.where(lane < HEAD_DIM, r0[:, 0:128], r1[:, 0:128])
+            within_dot[at, cols] = jnp.where(lane < HEAD_DIM, r0[:, 128:256] + q0, r1[:, 128:256] + q1)
+        return 0
+
+    halo_copies = [
+        remote(
+            proj.at[(k + 1) * length - 16 : (k + 1) * length, :],
+            halo.at[k],
+            halo_send.at[k],
+            halo_recv.at[k],
+            {"ctx": me + 1},
+        )
+        for k in range(2)
+    ]
+    for load in loads:
+        load.wait()
+    for c in (0, 1):
+        near(c)
+        forward(c)
+        distant(c)
+
+    @pl.when(me + 1 < count)
+    def _():
+        for copy in halo_copies:
+            copy.start()
+
+    convolve_all(1)
+    states_all(1)
+    score_all(1)
+    lax.fori_loop(0, half, functools.partial(mixing, 1), 0)
+    forward(2)
+    lax.fori_loop(half, pairs, functools.partial(mixing, 1), 0)
+    near(2)
+    distant(2)
+    near(3)
+    forward(3)
+    distant(3)
+
+    out_half = p_near.shape[2]
+    w_far = weight.at[0:width, 0:out_half]
+    w_near = weight.at[width : 2 * width, 0:out_half]
+    load_far = pltpu.make_async_copy(w_out.at[:, lanes((1 - chip) * out_half, out_half)], w_far, w_sem.at[3])
+    load_near = pltpu.make_async_copy(w_out.at[:, lanes(chip * out_half, out_half)], w_near, w_sem.at[4])
+    load_far.start()
+    load_near.start()
+
+    @pl.when(me > 0)
+    def _():
+        for copy in halo_copies:
+            copy.wait_recv()
+
+    convolve_all(0)
+    states_all(0)
+
+    mine = odd * half
+    others = (1 - odd) * half
+    pair_copies = [
+        remote(total.at[pl.ds(others, half)], pair_total, pair_send.at[0], pair_recv.at[0], {"ctx": partner}),
+        remote(rows.at[pl.ds(others, half)], pair_rows, pair_send.at[1], pair_recv.at[1], {"ctx": partner}),
+    ]
+    for copy in pair_copies:
+        copy.start()
+    score_all(0)
+    lax.fori_loop(0, pairs, functools.partial(mixing, 0), 0)
+    for copy in pair_copies:
+        copy.wait_recv()
+
+    chain_copies = [
+        remote(chain_out.at[i], chain_in.at[i], chain_send.at[i], chain_recv.at[i], {"ctx": me + 2})
+        for i in range(half)
+    ]
+    give_copies = [
+        remote(give.at[i], entry.at[mine + i], give_send.at[i], give_recv.at[i], {"ctx": partner})
+        for i in range(half)
+    ]
+    first_here = odd == 0
+    for i in range(half):
+
+        @pl.when(me >= 2)
+        def _(i=i):
+            chain_copies[i].wait_recv()
+
+        arrived, arrived_dot = chain_in[i, 0].astype(F32), chain_in[i, 1].astype(F32)
+        own, own_dot = total[mine + i, 0].astype(F32), total[mine + i, 1].astype(F32)
+        their, their_dot = pair_total[i, 0].astype(F32), pair_total[i, 1].astype(F32)
+        own_rows, their_rows = rows[mine + i], pair_rows[i]
+        early_rows = jnp.where(first_here, own_rows, their_rows)
+        late_rows = jnp.where(first_here, their_rows, own_rows)
+        retain = jnp.exp(early_rows[0:1])
+        middle = retain * arrived + jnp.where(first_here, own, their)
+        middle_dot = retain * (arrived_dot + early_rows[1:2] * arrived) + jnp.where(
+            first_here, own_dot, their_dot
+        )
+        retain = jnp.exp(late_rows[0:1])
+        chain_out[i, 0] = (retain * middle + jnp.where(first_here, their, own)).astype(BF16)
+        chain_out[i, 1] = (
+            retain * (middle_dot + late_rows[1:2] * middle) + jnp.where(first_here, their_dot, own_dot)
+        ).astype(BF16)
+
+        @pl.when(me + 2 < count)
+        def _(i=i):
+            chain_copies[i].start()
+
+        give[i, 0] = jnp.where(first_here, middle, arrived).astype(BF16)
+        give[i, 1] = jnp.where(first_here, middle_dot, arrived_dot).astype(BF16)
+        give_copies[i].start()
+        entry[mine + i, 0] = jnp.where(first_here, arrived, middle).astype(BF16)
+        entry[mine + i, 1] = jnp.where(first_here, arrived_dot, middle_dot).astype(BF16)
+
+    def finish(p, _):
+        cols = lanes(p * 128, 128)
+        gain = wide[length : length + 1, cols]
+        now, now_dot = entry[p, 0], entry[p, 1]
+        for b in range(blocks):
+            at = slice(b * SPAN, (b + 1) * SPAN)
+            end = slice((b + 1) * SPAN - 1, (b + 1) * SPAN)
+            reader = bc[at, state_len : 2 * state_len]
+            reader_dot = bc_dot[at, state_len : 2 * state_len]
+            read = jnp.dot(reader, jnp.concatenate([now, now_dot], 1), preferred_element_type=F32)
+            moved = jnp.dot(reader_dot, now, preferred_element_type=F32)
+            grown = jnp.exp(wide[at, cols])
+            plain = read[:, 0:128]
+            inner[at, cols] = (
+                within[at, cols] + grown * plain + gain * x[at, cols].astype(F32)
+            ).astype(BF16)
+            inner[length + b * SPAN : length + (b + 1) * SPAN, cols] = (
+                within_dot[at, cols]
+                + grown * (read[:, 128:256] + moved + wide_dot[at, cols] * plain)
+                + gain * x_dot[at, cols].astype(F32)
+            ).astype(BF16)
+            if b + 1 < blocks:
+                retain = jnp.exp(wide[end, cols])
+                old, old_dot = now.astype(F32), now_dot.astype(F32)
+                now = (retain * old + state[b, :, cols]).astype(BF16)
+                now_dot = (
+                    retain * (old_dot + wide_dot[end, cols] * old) + state_dot[b, :, cols]
+                ).astype(BF16)
+        return 0
+
+    lax.fori_loop(mine, mine + half, finish, 0)
+    back_copies = [
+        remote(give.at[i], entry.at[others + i], give_send.at[i], give_recv.at[i], {"ctx": partner})
+        for i in range(half)
+    ]
+    for i in range(half):
+        back_copies[i].wait_recv()
+    lax.fori_loop(others, others + half, finish, 0)
+
+    @pl.when(me + 1 < count)
+    def _():
+        for copy in halo_copies:
+            copy.wait_send()
+
+    keep = lanes(core * feat, feat)
+    other_half = lanes((1 - core) * feat, feat)
+    parts = 2 * length // SPAN
+
+    def part(r):
+        return slice(r * SPAN, (r + 1) * SPAN)
+
+    a_copies = [
+        remote(proj.at[part(r), other_half], r_far.at[r], a_send.at[r], a_recv.at[r], {"head": sib})
+        for r in range(parts)
+    ]
+    x_copies = [
+        remote(s_far.at[r], r_x.at[r], x_send.at[r], x_recv.at[r], {"head": far}) for r in range(parts)
+    ]
+    b_copies = [
+        remote(p_near.at[r, :, other_half], r_near.at[r], b_send.at[r], b_recv.at[r], {"head": sib})
+        for r in range(parts)
+    ]
+
+    def pass_on(r):
+        a_copies[r].wait_recv()
+        s_far[r] = (proj[part(r), keep].astype(F32) + r_far[r].astype(F32)).astype(BF16)
+        x_copies[r].start()
+
+    load_far.wait()
+    load_near.wait()
+    for r in range(parts):
+
+        def far_tile(j, _, r=r):
+            cols = lanes(j * 256, 256)
+            proj[part(r), cols] = jnp.dot(
+                inner[part(r), :], weight[0:width, cols], preferred_element_type=F32
+            ).astype(BF16)
+            return 0
+
+        lax.fori_loop(0, out_half // 256, far_tile, 0)
+        a_copies[r].start()
+        if r > 0:
+            pass_on(r - 1)
+    for r in range(parts):
+
+        def near_tile(j, _, r=r):
+            cols = lanes(j * 256, 256)
+            p_near[r, :, cols] = jnp.dot(
+                inner[part(r), :], weight[width : 2 * width, cols], preferred_element_type=F32
+            ).astype(BF16)
+            return 0
+
+        lax.fori_loop(0, out_half // 256, near_tile, 0)
+        b_copies[r].start()
+        if r == 0:
+            pass_on(parts - 1)
+    for r in range(parts):
+        b_copies[r].wait_recv()
+        x_copies[r].wait_recv()
+        summed = p_near[r, :, keep].astype(F32) + r_near[r].astype(F32) + r_x[r].astype(F32)
+        ref, at = (out, r) if r < parts // 2 else (out_dot, r - parts // 2)
+        ref[part(at), :] = summed.astype(BF16)
+
+    for copy in far_copies + sib_copies + fwd_copies + pair_copies + give_copies:
+        copy.wait_send()
+    for copy in a_copies + x_copies + b_copies:
+        copy.wait_send()
+
+    @pl.when(me + 2 < count)
+    def _():
+        for copy in chain_copies:
+            copy.wait_send()
+
+
+def fused_on_device(
+    tokens, tangent_tokens, log_decay, tangent_decay, w_inner, w_bmat, w_cmat,
+    conv_inner, conv_bc, skip_gain, w_out,
+):
+    length, feat = tokens.shape
+    depth, width = w_inner.shape
+    state_len = w_bmat.shape[1]
+    full = width + 2 * state_len
+    out_half = w_out.shape[1] // 2
+    blocks = length // SPAN
+    parts = 2 * blocks
+    pairs = width // 128
+    half = pairs // 2
+    vmem = pl.BlockSpec(memory_space=pltpu.VMEM)
+    anywhere = pl.BlockSpec(memory_space=pl.ANY)
+    dma = pltpu.SemaphoreType.DMA
+    piece = (2, state_len, 128)
+
+    def bf16(*shape):
+        return pltpu.VMEM(shape, BF16)
+
+    def f32(*shape):
+        return pltpu.VMEM(shape, F32)
+
+    result = jax.ShapeDtypeStruct((length, feat), BF16)
+    return pl.pallas_call(
+        layer_kernel,
+        out_shape=(result, result),
+        in_specs=[vmem] * 4 + [anywhere] * 3 + [vmem] * 3 + [anywhere],
+        out_specs=(vmem, vmem),
+        scratch_shapes=[
+            bf16(3, 2 * length, feat),
+            f32(SPAN + 16, full),
+            bf16(depth, full),
+            bf16(2 * length, full),
+            bf16(2 * length, width),
+            bf16(2, 16, full),
+            f32(2, 16 + SPAN, 128),
+            f32(2, 128, length),
+            f32(length + 8, 128),
+            f32(length, 128),
+            f32(blocks, 128, SPAN),
+            f32(blocks, 128, SPAN),
+            f32(length + 8, width),
+            f32(length, width),
+            bf16(length, width),
+            bf16(length, width),
+            bf16(length, 2 * state_len),
+            bf16(length, 2 * state_len),
+            f32(blocks, SPAN, SPAN),
+            f32(blocks, SPAN, SPAN),
+            f32(length, width),
+            f32(length, width),
+            f32(blocks, state_len, width),
+            f32(blocks, state_len, width),
+            bf16(pairs, *piece),
+            f32(pairs, 8, 128),
+            bf16(half, *piece),
+            f32(half, 8, 128),
+            bf16(half, *piece),
+            bf16(half, *piece),
+            bf16(half, *piece),
+            bf16(pairs, *piece),
+            bf16(parts, SPAN, out_half),
+        ]
+        + [bf16(parts, SPAN, feat)] * 4
+        + [dma((5,))]
+        + [dma((4,))] * 6
+        + [dma((2,))] * 4
+        + [dma((half,))] * 4
+        + [dma((parts,))] * 6,
+        compiler_params=pltpu.CompilerParams(
+            collective_id=0, has_side_effects=True, vmem_limit_bytes=VMEM_LIMIT
+        ),
+        name="layer",
+    )(
+        tokens, tangent_tokens, log_decay.T, tangent_decay.T, w_inner, w_bmat, w_cmat,
+        conv_inner, conv_bc, skip_gain.reshape(1, -1), w_out,
+    )
 
 
 def shifted(block, axis, distance):
@@ -188,6 +768,7 @@
         P("head", None),
     )
     out_specs = (P("ctx", "head"), P("ctx", "head"))
+    fits = mesh.shape["head"] == 4 and mesh.shape["ctx"] % 2 == 0
     return jax.shard_map(
-        on_device, mesh=mesh, in_specs=in_specs, out_specs=out_specs, check_vma=False
-    )
+        fused_on_device if fits else on_device, mesh=mesh, in_specs=in_specs, out_specs=out_specs, check_vma=False
+    )

time: 377 us -> 115 us (0.31)
  waiting for transfers between devices: 188 us -> 0 us
  Pallas kernels: 0 us -> 110 us
  local copies, waits for them, and re-layouts: 54.8 us -> 3.96 us
  matrix products: 44.1 us -> 0 us
  other arithmetic: 35.5 us -> 0 us
  blocking collectives: 35 us -> 0 us
  between operations: 14.5 us -> 0.64 us
    all_gather x3 -> x0, waiting for transfers between devices: 131 us -> none  [the longest x2 96.9 us: carried_in(): gathered = jax.tree.map(lambda a: lax.all_gather(a, axis), part)]
    pallas_call x0 -> x1, Pallas kernels: none -> 110 us  [fused_on_device(): pl.pallas_call(layer_kernel, out_shape=(result, result), in_specs=[vmem]...]
    unnamed x5 -> x0, waiting for transfers between devices: 53.2 us -> none
    dot_general x19 -> x0, matrix products: 44.1 us -> none  [the longest x3 12.7 us: span_parts(): jnp.einsum('hts,shp->thp', mixing, inputs, preferred_element_type=jnp.flo...]
    all_gather x2 -> x0, blocking collectives: 35 us -> none  [carried_in(): gathered = jax.tree.map(lambda a: lax.all_gather(a, axis), part)]
    add x9 -> x0, other arithmetic: 14.7 us -> none  [the longest x7 12.8 us: combine(): retain * (early_tangent + late_slope * early_state) + late_tangent]
    slice x15 -> x0, local copies, waits for them, and re-layouts: 12.8 us -> none  [the longest x4 7.29 us: separate(): inputs = values[:, :width].reshape(blocks, SPAN, heads_here, HEAD_DIM)]
    convert_element_type x4 -> x0, local copies, waits for them, and re-layouts: 11.4 us -> none  [finish(): skip_gain[None, :, None] * inputs[position]]
  transfers between devices with their start and end apart: 5 -> 0, of which waited for: 5 -> 0; matrix products, arithmetic and copies ran while one was open for 12% -> 0% of each run, Pallas kernels for 0% -> 0%
where the time goes in v2:
time: 115 us
  Pallas kernels  110 us (96%)
  local copies, waits for them, and re-layouts  3.96 us (3%)
    pallas_call x1, Pallas kernels, fused_on_device(): pl.pallas_call(layer_kernel, out_shape=(result, result), in_specs=[vmem]...  110 us
    unnamed x2, local copies, waits for them, and re-layouts  3.96 us

profile of v2, /device:TPU:28, one launch (start us, length us, event | category | flops | bytes accessed | tf_op | source)
XLA Modules:
  0.0 115.0 jit_solution(9772770015334534554)
XLA Ops:
  0.6 110.4 %layer.1 = (bf16[512,640]{1,0:T(8,128)(2,1)}, bf16[512,640]{1,0:T(8,128)(2,1)}) custom-call(bf16[512,640]{1,0:T(8,128)(2,1)} %tok.1, bf16[512,640]{1,0:T(8,128)(2,1)} %tan.1, f32[20,512]{1,0:T(8,128)} %bitcast.3, f32[20,512]{1,0:T(8,128)} %bitcast.4, bf16[2560,1280]{1,0:T(8,128)(2,1)} %w_in.1, bf16[2560,128]{1,0:T(8,128)(2,1)} %w_b.1, ...), custom_call_target="tpu_custom_call" | custom-call | tf_op jit(solution)/shard_map/layer/pallas_call | solution.py:534
  111.0 2.0 %copy.15 = bf16[512,640]{1,0:T(8,128)(2,1)} copy(bf16[512,640]{1,0:T(8,128)(2,1)} %get-tuple-element.4) | data formatting | bytes 1310720
  113.0 2.0 %copy.16 = bf16[512,640]{1,0:T(8,128)(2,1)} copy(bf16[512,640]{1,0:T(8,128)(2,1)} %get-tuple-element.5) | data formatting | bytes 1310720

commit v3 on v2

--- a/solution.py
+++ b/solution.py
@@ -239,8 +239,8 @@
                 log, slope = wide[final, cols], wide_dot[final, cols]
                 retain = jnp.exp(log)
                 rows[p] = jnp.concatenate([last + log, last_dot + slope, jnp.zeros((6, 128), F32)], 0)
-                total[p, 0] = (retain * new + state[1, :, cols]).astype(BF16)
-                total[p, 1] = (retain * (new_dot + slope * new) + state_dot[1, :, cols]).astype(BF16)
+                total[0, p] = (retain * new + state[1, :, cols]).astype(BF16)
+                total[1, p] = (retain * (new_dot + slope * new) + state_dot[1, :, cols]).astype(BF16)
             return 0
 
         lax.fori_loop(0, pairs, states, 0)
@@ -339,63 +339,94 @@
 
     mine = odd * half
     others = (1 - odd) * half
+    def pair_copy(source, into, k):
+        return remote(source, into, pair_send.at[k], pair_recv.at[k], {"ctx": partner})
+
     pair_copies = [
-        remote(total.at[pl.ds(others, half)], pair_total, pair_send.at[0], pair_recv.at[0], {"ctx": partner}),
-        remote(rows.at[pl.ds(others, half)], pair_rows, pair_send.at[1], pair_recv.at[1], {"ctx": partner}),
+        pair_copy(total.at[0, pl.ds(others, half)], pair_total.at[0], 0),
+        pair_copy(rows.at[pl.ds(others, half)], pair_rows, 1),
+        pair_copy(total.at[1, pl.ds(others, half)], pair_total.at[1], 2),
     ]
     for copy in pair_copies:
         copy.start()
     score_all(0)
     lax.fori_loop(0, pairs, functools.partial(mixing, 0), 0)
-    for copy in pair_copies:
-        copy.wait_recv()
-
     chain_copies = [
-        remote(chain_out.at[i], chain_in.at[i], chain_send.at[i], chain_recv.at[i], {"ctx": me + 2})
-        for i in range(half)
+        [
+            remote(chain_out.at[k, i], chain_in.at[k, i], chain_send.at[k, i], chain_recv.at[k, i], {"ctx": me + 2})
+            for i in range(half)
+        ]
+        for k in range(2)
     ]
     give_copies = [
-        remote(give.at[i], entry.at[mine + i], give_send.at[i], give_recv.at[i], {"ctx": partner})
-        for i in range(half)
+        [
+            remote(give.at[k, i], entry.at[k, mine + i], give_send.at[k, i], give_recv.at[k, i], {"ctx": partner})
+            for i in range(half)
+        ]
+        for k in range(2)
+    ]
+    back_copies = [
+        [
+            remote(give.at[k, i], entry.at[k, others + i], give_send.at[k, i], give_recv.at[k, i], {"ctx": partner})
+            for i in range(half)
+        ]
+        for k in range(2)
     ]
     first_here = odd == 0
-    for i in range(half):
-
+
+    def ordered(own_part, their_part):
+        return (
+            jnp.where(first_here, own_part, their_part),
+            jnp.where(first_here, their_part, own_part),
+        )
+
+    def link(k, i):
         @pl.when(me >= 2)
-        def _(i=i):
-            chain_copies[i].wait_recv()
-
-        arrived, arrived_dot = chain_in[i, 0].astype(F32), chain_in[i, 1].astype(F32)
-        own, own_dot = total[mine + i, 0].astype(F32), total[mine + i, 1].astype(F32)
-        their, their_dot = pair_total[i, 0].astype(F32), pair_total[i, 1].astype(F32)
-        own_rows, their_rows = rows[mine + i], pair_rows[i]
-        early_rows = jnp.where(first_here, own_rows, their_rows)
-        late_rows = jnp.where(first_here, their_rows, own_rows)
-        retain = jnp.exp(early_rows[0:1])
-        middle = retain * arrived + jnp.where(first_here, own, their)
-        middle_dot = retain * (arrived_dot + early_rows[1:2] * arrived) + jnp.where(
-            first_here, own_dot, their_dot
-        )
-        retain = jnp.exp(late_rows[0:1])
-        chain_out[i, 0] = (retain * middle + jnp.where(first_here, their, own)).astype(BF16)
-        chain_out[i, 1] = (
-            retain * (middle_dot + late_rows[1:2] * middle) + jnp.where(first_here, their_dot, own_dot)
-        ).astype(BF16)
+        def _():
+            chain_copies[k][i].wait_recv()
+
+        early_rows, late_rows = ordered(rows[mine + i], pair_rows[i])
+        keep_early, keep_late = jnp.exp(early_rows[0:1]), jnp.exp(late_rows[0:1])
+        early, late = ordered(total[0, mine + i].astype(F32), pair_total[0, i].astype(F32))
+        arrived = chain_in[0, i].astype(F32)
+        middle = keep_early * arrived + early
+        leaving = keep_late * middle + late
+        if k == 1:
+            early, late = ordered(total[1, mine + i].astype(F32), pair_total[1, i].astype(F32))
+            slope_early, slope_late = early_rows[1:2], late_rows[1:2]
+            before = arrived
+            arrived = chain_in[1, i].astype(F32)
+            leaving = keep_early * (arrived + slope_early * before) + early
+            leaving, middle = keep_late * (leaving + slope_late * middle) + late, leaving
+        chain_out[k, i] = leaving.astype(BF16)
 
         @pl.when(me + 2 < count)
-        def _(i=i):
-            chain_copies[i].start()
-
-        give[i, 0] = jnp.where(first_here, middle, arrived).astype(BF16)
-        give[i, 1] = jnp.where(first_here, middle_dot, arrived_dot).astype(BF16)
-        give_copies[i].start()
-        entry[mine + i, 0] = jnp.where(first_here, arrived, middle).astype(BF16)
-        entry[mine + i, 1] = jnp.where(first_here, arrived_dot, middle_dot).astype(BF16)
+        def _():
+            chain_copies[k][i].start()
+
+        give[k, i] = jnp.where(first_here, middle, arrived).astype(BF16)
+        give_copies[k][i].start()
+        entry[k, mine + i] = jnp.where(first_here, arrived, middle).astype(BF16)
 
     def finish(p, _):
         cols = lanes(p * 128, 128)
         gain = wide[length : length + 1, cols]
-        now, now_dot = entry[p, 0], entry[p, 1]
+        now = entry[0, p]
+        for b in range(blocks):
+            at = slice(b * SPAN, (b + 1) * SPAN)
+            end = slice((b + 1) * SPAN - 1, (b + 1) * SPAN)
+            read = jnp.dot(bc[at, state_len : 2 * state_len], now, preferred_element_type=F32)
+            inner[at, cols] = (
+                within[at, cols] + jnp.exp(wide[at, cols]) * read + gain * x[at, cols].astype(F32)
+            ).astype(BF16)
+            if b + 1 < blocks:
+                now = (jnp.exp(wide[end, cols]) * now.astype(F32) + state[b, :, cols]).astype(BF16)
+        return 0
+
+    def finish_dot(p, _):
+        cols = lanes(p * 128, 128)
+        gain = wide[length : length + 1, cols]
+        now, now_dot = entry[0, p], entry[1, p]
         for b in range(blocks):
             at = slice(b * SPAN, (b + 1) * SPAN)
             end = slice((b + 1) * SPAN - 1, (b + 1) * SPAN)
@@ -403,14 +434,10 @@
             reader_dot = bc_dot[at, state_len : 2 * state_len]
             read = jnp.dot(reader, jnp.concatenate([now, now_dot], 1), preferred_element_type=F32)
             moved = jnp.dot(reader_dot, now, preferred_element_type=F32)
-            grown = jnp.exp(wide[at, cols])
-            plain = read[:, 0:128]
-            inner[at, cols] = (
-                within[at, cols] + grown * plain + gain * x[at, cols].astype(F32)
-            ).astype(BF16)
             inner[length + b * SPAN : length + (b + 1) * SPAN, cols] = (
                 within_dot[at, cols]
-                + grown * (read[:, 128:256] + moved + wide_dot[at, cols] * plain)
+                + jnp.exp(wide[at, cols])
+                * (read[:, 128:256] + moved + wide_dot[at, cols] * read[:, 0:128])
                 + gain * x_dot[at, cols].astype(F32)
             ).astype(BF16)
             if b + 1 < blocks:
@@ -422,20 +449,6 @@
                 ).astype(BF16)
         return 0
 
-    lax.fori_loop(mine, mine + half, finish, 0)
-    back_copies = [
-        remote(give.at[i], entry.at[others + i], give_send.at[i], give_recv.at[i], {"ctx": partner})
-        for i in range(half)
-    ]
-    for i in range(half):
-        back_copies[i].wait_recv()
-    lax.fori_loop(others, others + half, finish, 0)
-
-    @pl.when(me + 1 < count)
-    def _():
-        for copy in halo_copies:
-            copy.wait_send()
-
     keep = lanes(core * feat, feat)
     other_half = lanes((1 - core) * feat, feat)
     parts = 2 * length // SPAN
@@ -460,34 +473,63 @@
         s_far[r] = (proj[part(r), keep].astype(F32) + r_far[r].astype(F32)).astype(BF16)
         x_copies[r].start()
 
-    load_far.wait()
-    load_near.wait()
-    for r in range(parts):
-
-        def far_tile(j, _, r=r):
+    def far_terms(r):
+        def one(j, _):
             cols = lanes(j * 256, 256)
             proj[part(r), cols] = jnp.dot(
                 inner[part(r), :], weight[0:width, cols], preferred_element_type=F32
             ).astype(BF16)
             return 0
 
-        lax.fori_loop(0, out_half // 256, far_tile, 0)
+        lax.fori_loop(0, out_half // 256, one, 0)
         a_copies[r].start()
-        if r > 0:
-            pass_on(r - 1)
-    for r in range(parts):
-
-        def near_tile(j, _, r=r):
+
+    def near_terms(r):
+        def one(j, _):
             cols = lanes(j * 256, 256)
             p_near[r, :, cols] = jnp.dot(
                 inner[part(r), :], weight[width : 2 * width, cols], preferred_element_type=F32
             ).astype(BF16)
             return 0
 
-        lax.fori_loop(0, out_half // 256, near_tile, 0)
+        lax.fori_loop(0, out_half // 256, one, 0)
         b_copies[r].start()
-        if r == 0:
-            pass_on(parts - 1)
+
+    pair_copies[0].wait_recv()
+    pair_copies[1].wait_recv()
+    for i in range(half):
+        link(0, i)
+    lax.fori_loop(mine, mine + half, finish, 0)
+    load_far.wait()
+    load_near.wait()
+
+    @pl.when(me + 1 < count)
+    def _():
+        for copy in halo_copies:
+            copy.wait_send()
+
+    for i in range(half):
+        back_copies[0][i].wait_recv()
+    lax.fori_loop(others, others + half, finish, 0)
+    far_terms(0)
+    far_terms(1)
+    pass_on(0)
+    pair_copies[2].wait_recv()
+    near_terms(0)
+    pass_on(1)
+    for i in range(half):
+        link(1, i)
+    lax.fori_loop(mine, mine + half, finish_dot, 0)
+    for i in range(half):
+        back_copies[1][i].wait_recv()
+    lax.fori_loop(others, others + half, finish_dot, 0)
+    far_terms(2)
+    far_terms(3)
+    pass_on(2)
+    near_terms(1)
+    pass_on(3)
+    near_terms(2)
+    near_terms(3)
     for r in range(parts):
         b_copies[r].wait_recv()
         x_copies[r].wait_recv()
@@ -495,15 +537,20 @@
         ref, at = (out, r) if r < parts // 2 else (out_dot, r - parts // 2)
         ref[part(at), :] = summed.astype(BF16)
 
-    for copy in far_copies + sib_copies + fwd_copies + pair_copies + give_copies:
+    for copy in far_copies + sib_copies + fwd_copies + pair_copies + give_copies[0] + give_copies[1]:
         copy.wait_send()
     for copy in a_copies + x_copies + b_copies:
         copy.wait_send()
 
     @pl.when(me + 2 < count)
     def _():
-        for copy in chain_copies:
+        for copy in chain_copies[0] + chain_copies[1]:
             copy.wait_send()
+
+
+def place_kernel(values, values_dot, out, out_dot):
+    out[...] = values[...]
+    out_dot[...] = values_dot[...]
 
 
 def fused_on_device(
@@ -522,7 +569,7 @@
     vmem = pl.BlockSpec(memory_space=pltpu.VMEM)
     anywhere = pl.BlockSpec(memory_space=pl.ANY)
     dma = pltpu.SemaphoreType.DMA
-    piece = (2, state_len, 128)
+    piece = (state_len, 128)
 
     def bf16(*shape):
         return pltpu.VMEM(shape, BF16)
@@ -531,7 +578,7 @@
         return pltpu.VMEM(shape, F32)
 
     result = jax.ShapeDtypeStruct((length, feat), BF16)
-    return pl.pallas_call(
+    outputs = pl.pallas_call(
         layer_kernel,
         out_shape=(result, result),
         in_specs=[vmem] * 4 + [anywhere] * 3 + [vmem] * 3 + [anywhere],
@@ -561,21 +608,22 @@
             f32(length, width),
             f32(blocks, state_len, width),
             f32(blocks, state_len, width),
-            bf16(pairs, *piece),
+            bf16(2, pairs, *piece),
             f32(pairs, 8, 128),
-            bf16(half, *piece),
+            bf16(2, half, *piece),
             f32(half, 8, 128),
-            bf16(half, *piece),
-            bf16(half, *piece),
-            bf16(half, *piece),
-            bf16(pairs, *piece),
+            bf16(2, half, *piece),
+            bf16(2, half, *piece),
+            bf16(2, half, *piece),
+            bf16(2, pairs, *piece),
             bf16(parts, SPAN, out_half),
         ]
         + [bf16(parts, SPAN, feat)] * 4
         + [dma((5,))]
         + [dma((4,))] * 6
-        + [dma((2,))] * 4
-        + [dma((half,))] * 4
+        + [dma((2,))] * 2
+        + [dma((3,))] * 2
+        + [dma((2, half))] * 4
         + [dma((parts,))] * 6,
         compiler_params=pltpu.CompilerParams(
             collective_id=0, has_side_effects=True, vmem_limit_bytes=VMEM_LIMIT
@@ -585,6 +633,14 @@
         tokens, tangent_tokens, log_decay.T, tangent_decay.T, w_inner, w_bmat, w_cmat,
         conv_inner, conv_bc, skip_gain.reshape(1, -1), w_out,
     )
+    return pl.pallas_call(
+        place_kernel,
+        out_shape=(result, result),
+        in_specs=[vmem, vmem],
+        out_specs=(vmem, vmem),
+        compiler_params=pltpu.CompilerParams(vmem_limit_bytes=16 * 1024 * 1024),
+        name="place",
+    )(*outputs)
 
 
 def shifted(block, axis, distance):

time: 115 us -> 106 us (0.922)
  Pallas kernels: 110 us -> 103 us
  local copies, waits for them, and re-layouts: 3.96 us -> 2.17 us
    pallas_call x1, Pallas kernels: 110 us -> 102 us  [fused_on_device(): pl.pallas_call(layer_kernel, out_shape=(result, result), in_specs=[vmem]...]
    unnamed x2 -> x4, local copies, waits for them, and re-layouts: 3.96 us -> 2.17 us
    pallas_call x0 -> x1, Pallas kernels: none -> 1.15 us  [fused_on_device(): pl.pallas_call(place_kernel, out_shape=(result, result), in_specs=[vmem,...]
where the time goes in v3:
time: 106 us
  Pallas kernels  103 us (97%)
  local copies, waits for them, and re-layouts  2.17 us (2%)
    pallas_call x1, Pallas kernels, fused_on_device(): pl.pallas_call(layer_kernel, out_shape=(result, result), in_specs=[vmem]...  102 us
    unnamed x4, local copies, waits for them, and re-layouts  2.17 us

profile of v3, /device:TPU:28, one launch (start us, length us, event | category | flops | bytes accessed | tf_op | source)
XLA Modules:
  0.0 105.8 jit_solution(11791181807400120921)
XLA Ops:
  0.6 101.8 %layer.1 = (bf16[512,640]{1,0:T(8,128)(2,1)}, bf16[512,640]{1,0:T(8,128)(2,1)}) custom-call(bf16[512,640]{1,0:T(8,128)(2,1)} %tok.1, bf16[512,640]{1,0:T(8,128)(2,1)} %tan.1, f32[20,512]{1,0:T(8,128)} %bitcast.3, f32[20,512]{1,0:T(8,128)} %bitcast.4, bf16[2560,1280]{1,0:T(8,128)(2,1)} %w_in.1, bf16[2560,128]{1,0:T(8,128)(2,1)} %w_b.1, ...), custom_call_target="tpu_custom_call" | custom-call | tf_op jit(solution)/shard_map/layer/pallas_call | solution.py:581
  102.5 0.0 copy-start
  102.5 1.1 %copy-done = bf16[512,640]{1,0:T(8,128)(2,1)S(1)} copy-done((bf16[512,640]{1,0:T(8,128)(2,1)S(1)}, bf16[512,640]{1,0:T(8,128)(2,1)}, u32[]{:S(2)}) %copy-start) | copy-done | bytes 655384
  103.6 0.0 copy-start.1
  103.6 1.1 %copy-done.1 = bf16[512,640]{1,0:T(8,128)(2,1)S(1)} copy-done((bf16[512,640]{1,0:T(8,128)(2,1)S(1)}, bf16[512,640]{1,0:T(8,128)(2,1)}, u32[]{:S(2)}) %copy-start.1) | copy-done | bytes 655384
  104.6 1.2 %place.1 = (bf16[512,640]{1,0:T(8,128)(2,1)}, bf16[512,640]{1,0:T(8,128)(2,1)}) custom-call(bf16[512,640]{1,0:T(8,128)(2,1)S(1)} %copy-done, bf16[512,640]{1,0:T(8,128)(2,1)S(1)} %copy-done.1), custom_call_target="tpu_custom_call" | custom-call | tf_op jit(solution)/shard_map/place/pallas_call | solution.py:636
Async XLA Ops:
  102.5 1.1 %copy-start = (bf16[512,640]{1,0:T(8,128)(2,1)S(1)}, bf16[512,640]{1,0:T(8,128)(2,1)}, u32[]{:S(2)}) copy-start(bf16[512,640]{1,0:T(8,128)(2,1)} %get-tuple-element.4.values) | copy-start | bytes 1966084
  103.6 1.1 %copy-start.1 = (bf16[512,640]{1,0:T(8,128)(2,1)S(1)}, bf16[512,640]{1,0:T(8,128)(2,1)}, u32[]{:S(2)}) copy-start(bf16[512,640]{1,0:T(8,128)(2,1)} %get-tuple-element.5.values_dot) | copy-start | bytes 1966084

commit v4 on v3

--- a/solution.py
+++ b/solution.py
@@ -32,8 +32,8 @@
     halo, padded, pad_dec, cum, cum_dot, cum_t, cum_dot_t, wide, wide_dot, x, x_dot, bc, bc_dot,
     score, score_dot, within, within_dot, state, state_dot,
     total, rows, pair_total, pair_rows, chain_in, chain_out, give, entry,
-    p_near, r_far, s_far, r_x, r_near,
-    w_sem, sib_send, sib_recv, far_send, far_recv, fwd_send, fwd_recv,
+    p_near, r_far, s_far, r_x, r_near, staged, own_tok, own_tan,
+    store_sem, w_sem, sib_send, sib_recv, far_send, far_recv, fwd_send, fwd_recv,
     halo_send, halo_recv, pair_send, pair_recv, chain_send, chain_recv, give_send, give_recv,
     a_send, a_recv, x_send, x_recv, b_send, b_recv,
 ):
@@ -57,6 +57,8 @@
     lane = lax.broadcasted_iota(jnp.int32, (1, 128), 1)
 
     loads = [
+        pltpu.make_async_copy(tok, own_tok, w_sem.at[5]),
+        pltpu.make_async_copy(tan, own_tan, w_sem.at[6]),
         pltpu.make_async_copy(w_in, weight.at[:, 0:width], w_sem.at[0]),
         pltpu.make_async_copy(w_b, weight.at[:, width : width + state_len], w_sem.at[1]),
         pltpu.make_async_copy(w_c, weight.at[:, width + state_len :], w_sem.at[2]),
@@ -83,6 +85,10 @@
         k, start, size = chunks[c]
         return (tok, tan)[k].at[start : start + size]
 
+    def own_values(c):
+        k, start, size = chunks[c]
+        return (own_tok, own_tan)[k][start : start + size, :]
+
     def span(c):
         k, start, size = chunks[c]
         return slice(k * length + start, k * length + start + size)
@@ -113,7 +119,7 @@
         def one(j, _):
             cols = lanes(j * 256, 256)
             acc[0:size, cols] = jnp.dot(
-                own(c)[...], weight[block(head), cols], preferred_element_type=F32
+                own_values(c), weight[block(head), cols], preferred_element_type=F32
             ) + jnp.dot(held[0, span(c), :], weight[block(sib), cols], preferred_element_type=F32)
             return 0
 
@@ -180,10 +186,10 @@
 
     lax.fori_loop(0, pairs, expand, 0)
 
-    def convolve(b, cols, kernel, into, into_dot, to):
+    def convolve(b, wanted, cols, kernel, into, into_dot, to):
         start = b * SPAN
         convs = []
-        for k in range(2):
+        for k in range(1 + max(wanted)):
             if b == 0:
                 padded[k, 0:16, :] = halo[k, :, cols].astype(F32)
             else:
@@ -194,53 +200,60 @@
                 summed = summed + kernel[tap : tap + 1, :] * padded[k, 13 + tap : 13 + tap + SPAN, :]
             convs.append(summed)
         gate = 1.0 / (1.0 + jnp.exp(-convs[0]))
-        into[start : start + SPAN, to] = (convs[0] * gate).astype(BF16)
-        into_dot[start : start + SPAN, to] = (
-            convs[1] * (gate * (1.0 + convs[0] * (1.0 - gate)))
-        ).astype(BF16)
-
-    def convolve_all(b):
+        if 0 in wanted:
+            into[start : start + SPAN, to] = (convs[0] * gate).astype(BF16)
+        if 1 in wanted:
+            into_dot[start : start + SPAN, to] = (
+                convs[1] * (gate * (1.0 + convs[0] * (1.0 - gate)))
+            ).astype(BF16)
+
+    def convolve_all(b, wanted):
         for k in range(2):
             part = slice(k * state_len, (k + 1) * state_len)
             convolve(
-                b, slice(width + k * state_len, width + (k + 1) * state_len), conv_bc[:, part], bc, bc_dot, part
+                b, wanted, slice(width + k * state_len, width + (k + 1) * state_len), conv_bc[:, part], bc, bc_dot, part
             )
 
         def convolve_inner(p, _):
             cols = lanes(p * 128, 128)
-            convolve(b, cols, conv_in[:, cols], x, x_dot, cols)
+            convolve(b, wanted, cols, conv_in[:, cols], x, x_dot, cols)
             return 0
 
         lax.fori_loop(0, pairs, convolve_inner, 0)
 
-    def states_all(b):
+    def states_all(b, wanted):
         at = slice(b * SPAN, (b + 1) * SPAN)
         end = slice((b + 1) * SPAN - 1, (b + 1) * SPAN)
+        final = slice(2 * SPAN - 1, 2 * SPAN)
         writer_t = bc[at, 0:state_len].T
-        writer_dot_t = bc_dot[at, 0:state_len].T
+        writer_dot_t = bc_dot[at, 0:state_len].T if 1 in wanted else None
 
         def states(p, _):
             cols = lanes(p * 128, 128)
             last, last_dot = wide[end, cols], wide_dot[end, cols]
+            log, slope = wide[final, cols], wide_dot[final, cols]
+            retain = jnp.exp(log)
             remaining = jnp.exp(last - wide[at, cols])
             values = x[at, cols].astype(F32)
             scaled = (values * remaining).astype(BF16)
-            scaled_dot = (
-                (x_dot[at, cols].astype(F32) + values * (last_dot - wide_dot[at, cols])) * remaining
-            ).astype(BF16)
-            new = jnp.dot(writer_t, scaled, preferred_element_type=F32)
-            new_dot = jnp.dot(writer_t, scaled_dot, preferred_element_type=F32) + jnp.dot(
-                writer_dot_t, scaled, preferred_element_type=F32
-            )
-            state[b, :, cols] = new
-            state_dot[b, :, cols] = new_dot
-            if b == 0:
-                final = slice(2 * SPAN - 1, 2 * SPAN)
-                log, slope = wide[final, cols], wide_dot[final, cols]
-                retain = jnp.exp(log)
-                rows[p] = jnp.concatenate([last + log, last_dot + slope, jnp.zeros((6, 128), F32)], 0)
-                total[0, p] = (retain * new + state[1, :, cols]).astype(BF16)
-                total[1, p] = (retain * (new_dot + slope * new) + state_dot[1, :, cols]).astype(BF16)
+            if 0 in wanted:
+                new = jnp.dot(writer_t, scaled, preferred_element_type=F32)
+                state[b, :, cols] = new
+                if b == 0:
+                    rows[p] = jnp.concatenate([last + log, last_dot + slope, jnp.zeros((6, 128), F32)], 0)
+                    total[0, p] = (retain * new + state[1, :, cols]).astype(BF16)
+            if 1 in wanted:
+                scaled_dot = (
+                    (x_dot[at, cols].astype(F32) + values * (last_dot - wide_dot[at, cols])) * remaining
+                ).astype(BF16)
+                new_dot = jnp.dot(writer_t, scaled_dot, preferred_element_type=F32) + jnp.dot(
+                    writer_dot_t, scaled, preferred_element_type=F32
+                )
+                state_dot[b, :, cols] = new_dot
+                if b == 0:
+                    total[1, p] = (
+                        retain * (new_dot + slope * state[0, :, cols]) + state_dot[1, :, cols]
+                    ).astype(BF16)
             return 0
 
         lax.fori_loop(0, pairs, states, 0)
@@ -297,46 +310,7 @@
         )
         for k in range(2)
     ]
-    for load in loads:
-        load.wait()
-    for c in (0, 1):
-        near(c)
-        forward(c)
-        distant(c)
-
-    @pl.when(me + 1 < count)
-    def _():
-        for copy in halo_copies:
-            copy.start()
-
-    convolve_all(1)
-    states_all(1)
-    score_all(1)
-    lax.fori_loop(0, half, functools.partial(mixing, 1), 0)
-    forward(2)
-    lax.fori_loop(half, pairs, functools.partial(mixing, 1), 0)
-    near(2)
-    distant(2)
-    near(3)
-    forward(3)
-    distant(3)
-
     out_half = p_near.shape[2]
-    w_far = weight.at[0:width, 0:out_half]
-    w_near = weight.at[width : 2 * width, 0:out_half]
-    load_far = pltpu.make_async_copy(w_out.at[:, lanes((1 - chip) * out_half, out_half)], w_far, w_sem.at[3])
-    load_near = pltpu.make_async_copy(w_out.at[:, lanes(chip * out_half, out_half)], w_near, w_sem.at[4])
-    load_far.start()
-    load_near.start()
-
-    @pl.when(me > 0)
-    def _():
-        for copy in halo_copies:
-            copy.wait_recv()
-
-    convolve_all(0)
-    states_all(0)
-
     mine = odd * half
     others = (1 - odd) * half
     def pair_copy(source, into, k):
@@ -347,10 +321,6 @@
         pair_copy(rows.at[pl.ds(others, half)], pair_rows, 1),
         pair_copy(total.at[1, pl.ds(others, half)], pair_total.at[1], 2),
     ]
-    for copy in pair_copies:
-        copy.start()
-    score_all(0)
-    lax.fori_loop(0, pairs, functools.partial(mixing, 0), 0)
     chain_copies = [
         [
             remote(chain_out.at[k, i], chain_in.at[k, i], chain_send.at[k, i], chain_recv.at[k, i], {"ctx": me + 2})
@@ -495,10 +465,56 @@
         lax.fori_loop(0, out_half // 256, one, 0)
         b_copies[r].start()
 
+    for load in loads:
+        load.wait()
+    for c in (0, 1):
+        near(c)
+        forward(c)
+        distant(c)
+
+    @pl.when(me + 1 < count)
+    def _():
+        for copy in halo_copies:
+            copy.start()
+
+    convolve_all(1, (0, 1))
+    states_all(1, (0, 1))
+    score_all(1)
+    lax.fori_loop(0, half, functools.partial(mixing, 1), 0)
+    forward(2)
+    lax.fori_loop(half, pairs, functools.partial(mixing, 1), 0)
+    near(2)
+    distant(2)
+
+    @pl.when(me > 0)
+    def _():
+        for copy in halo_copies:
+            copy.wait_recv()
+
+    convolve_all(0, (0,))
+    states_all(0, (0,))
+    pair_copies[0].start()
+    pair_copies[1].start()
+    near(3)
     pair_copies[0].wait_recv()
     pair_copies[1].wait_recv()
     for i in range(half):
         link(0, i)
+    forward(3)
+    distant(3)
+
+    w_far = weight.at[0:width, 0:out_half]
+    w_near = weight.at[width : 2 * width, 0:out_half]
+    load_far = pltpu.make_async_copy(w_out.at[:, lanes((1 - chip) * out_half, out_half)], w_far, w_sem.at[3])
+    load_near = pltpu.make_async_copy(w_out.at[:, lanes(chip * out_half, out_half)], w_near, w_sem.at[4])
+    load_far.start()
+    load_near.start()
+
+    convolve_all(0, (1,))
+    states_all(0, (1,))
+    pair_copies[2].start()
+    score_all(0)
+    lax.fori_loop(0, pairs, functools.partial(mixing, 0), 0)
     lax.fori_loop(mine, mine + half, finish, 0)
     load_far.wait()
     load_near.wait()
@@ -530,17 +546,25 @@
     pass_on(3)
     near_terms(2)
     near_terms(3)
+    stores = [
+        pltpu.make_async_copy(
+            staged.at[r], (out if r < parts // 2 else out_dot).at[part(r % (parts // 2))], store_sem.at[r]
+        )
+        for r in range(parts)
+    ]
     for r in range(parts):
         b_copies[r].wait_recv()
         x_copies[r].wait_recv()
         summed = p_near[r, :, keep].astype(F32) + r_near[r].astype(F32) + r_x[r].astype(F32)
-        ref, at = (out, r) if r < parts // 2 else (out_dot, r - parts // 2)
-        ref[part(at), :] = summed.astype(BF16)
+        staged[r] = summed.astype(BF16)
+        stores[r].start()
 
     for copy in far_copies + sib_copies + fwd_copies + pair_copies + give_copies[0] + give_copies[1]:
         copy.wait_send()
     for copy in a_copies + x_copies + b_copies:
         copy.wait_send()
+    for store in stores:
+        store.wait()
 
     @pl.when(me + 2 < count)
     def _():
@@ -548,9 +572,17 @@
             copy.wait_send()
 
 
-def place_kernel(values, values_dot, out, out_dot):
-    out[...] = values[...]
-    out_dot[...] = values_dot[...]
+def place_kernel(values, values_dot, out, out_dot, sem):
+    size = out.shape[0] // 4
+    copies = []
+    for k, (source, into) in enumerate(((values, out), (values_dot, out_dot))):
+        for i in range(4):
+            at = slice(i * size, (i + 1) * size)
+            copies.append(pltpu.make_async_copy(source.at[at], into.at[at], sem.at[4 * k + i]))
+    for copy in copies:
+        copy.start()
+    for copy in copies:
+        copy.wait()
 
 
 def fused_on_device(
@@ -581,8 +613,8 @@
     outputs = pl.pallas_call(
         layer_kernel,
         out_shape=(result, result),
-        in_specs=[vmem] * 4 + [anywhere] * 3 + [vmem] * 3 + [anywhere],
-        out_specs=(vmem, vmem),
+        in_specs=[anywhere] * 2 + [vmem] * 2 + [anywhere] * 3 + [vmem] * 3 + [anywhere],
+        out_specs=(anywhere, anywhere),
         scratch_shapes=[
             bf16(3, 2 * length, feat),
             f32(SPAN + 16, full),
@@ -618,8 +650,10 @@
             bf16(2, pairs, *piece),
             bf16(parts, SPAN, out_half),
         ]
-        + [bf16(parts, SPAN, feat)] * 4
-        + [dma((5,))]
+        + [bf16(parts, SPAN, feat)] * 5
+        + [bf16(length, feat)] * 2
+        + [dma((parts,))]
+        + [dma((7,))]
         + [dma((4,))] * 6
         + [dma((2,))] * 2
         + [dma((3,))] * 2
@@ -636,9 +670,10 @@
     return pl.pallas_call(
         place_kernel,
         out_shape=(result, result),
-        in_specs=[vmem, vmem],
-        out_specs=(vmem, vmem),
-        compiler_params=pltpu.CompilerParams(vmem_limit_bytes=16 * 1024 * 1024),
+        in_specs=[anywhere, anywhere],
+        out_specs=(anywhere, anywhere),
+        scratch_shapes=[dma((8,))],
+        compiler_params=pltpu.CompilerParams(vmem_limit_bytes=VMEM_LIMIT),
         name="place",
     )(*outputs)
 

time: 106 us -> 146 us (1.38)
  Pallas kernels: 103 us -> 144 us
  local copies, waits for them, and re-layouts: 2.17 us -> 0 us
    pallas_call x2, Pallas kernels: 103 us -> 144 us  [the longest x1 103 us: fused_on_device(): pl.pallas_call(layer_kernel, out_shape=(result, result), in_specs=[anywhe...]
    unnamed x4 -> x0, local copies, waits for them, and re-layouts: 2.17 us -> none
where the time goes in v4:
time: 146 us; the launch traced here: 145 us
  Pallas kernels  144 us (99%)
    pallas_call x1, Pallas kernels, fused_on_device(): pl.pallas_call(layer_kernel, out_shape=(result, result), in_specs=[anywhe...  103 us
    pallas_call x1, Pallas kernels, fused_on_device(): pl.pallas_call(place_kernel, out_shape=(result, result), in_specs=[anywhe...  40.9 us

profile of v4, /device:TPU:28, one launch (start us, length us, event | category | flops | bytes accessed | tf_op | source)
XLA Modules:
  0.0 144.8 jit_solution(17167724880204856217)
XLA Ops:
  0.6 103.3 %layer.1 = (bf16[512,640]{1,0:T(8,128)(2,1)}, bf16[512,640]{1,0:T(8,128)(2,1)}) custom-call(bf16[512,640]{1,0:T(8,128)(2,1)} %tok.1, bf16[512,640]{1,0:T(8,128)(2,1)} %tan.1, f32[20,512]{1,0:T(8,128)} %bitcast.3, f32[20,512]{1,0:T(8,128)} %bitcast.4, bf16[2560,1280]{1,0:T(8,128)(2,1)} %w_in.1, bf16[2560,128]{1,0:T(8,128)(2,1)} %w_b.1, ...), custom_call_target="tpu_custom_call" | custom-call | tf_op jit(solution)/shard_map/layer/pallas_call | solution.py:613
  103.9 40.9 %place.1 = (bf16[512,640]{1,0:T(8,128)(2,1)}, bf16[512,640]{1,0:T(8,128)(2,1)}) custom-call(bf16[512,640]{1,0:T(8,128)(2,1)} %get-tuple-element.4.values, bf16[512,640]{1,0:T(8,128)(2,1)} %get-tuple-element.5.values_dot), custom_call_target="tpu_custom_call" | custom-call | tf_op jit(solution)/shard_map/place/pallas_call | solution.py:670

commit v5 on v4

--- a/solution.py
+++ b/solution.py
@@ -498,8 +498,12 @@
     near(3)
     pair_copies[0].wait_recv()
     pair_copies[1].wait_recv()
-    for i in range(half):
-        link(0, i)
+
+    @pl.when(me < count // 2)
+    def _():
+        for i in range(half):
+            link(0, i)
+
     forward(3)
     distant(3)
 
@@ -513,8 +517,21 @@
     convolve_all(0, (1,))
     states_all(0, (1,))
     pair_copies[2].start()
+
+    @pl.when(me >= count // 2)
+    def _():
+        for i in range(half):
+            link(0, i)
+
     score_all(0)
     lax.fori_loop(0, pairs, functools.partial(mixing, 0), 0)
+    pair_copies[2].wait_recv()
+
+    @pl.when(me < count // 2)
+    def _():
+        for i in range(half):
+            link(1, i)
+
     lax.fori_loop(mine, mine + half, finish, 0)
     load_far.wait()
     load_near.wait()
@@ -530,11 +547,14 @@
     far_terms(0)
     far_terms(1)
     pass_on(0)
-    pair_copies[2].wait_recv()
     near_terms(0)
     pass_on(1)
-    for i in range(half):
-        link(1, i)
+
+    @pl.when(me >= count // 2)
+    def _():
+        for i in range(half):
+            link(1, i)
+
     lax.fori_loop(mine, mine + half, finish_dot, 0)
     for i in range(half):
         back_copies[1][i].wait_recv()
@@ -671,7 +691,7 @@
         place_kernel,
         out_shape=(result, result),
         in_specs=[anywhere, anywhere],
-        out_specs=(anywhere, anywhere),
+        out_specs=(vmem, vmem),
         scratch_shapes=[dma((8,))],
         compiler_params=pltpu.CompilerParams(vmem_limit_bytes=VMEM_LIMIT),
         name="place",

time: 146 us -> 104 us (0.71)
  Pallas kernels: 144 us -> 102 us
    pallas_call x1, Pallas kernels: 40.9 us -> 2.51 us  [fused_on_device(): pl.pallas_call(place_kernel, out_shape=(result, result), in_specs=[anywhe...]
    pallas_call x1, Pallas kernels: 103 us -> 99 us  [fused_on_device(): pl.pallas_call(layer_kernel, out_shape=(result, result), in_specs=[anywhe...]
where the time goes in v5:
time: 104 us; the launch traced here: 102 us
  Pallas kernels  102 us (98%)
    pallas_call x1, Pallas kernels, fused_on_device(): pl.pallas_call(layer_kernel, out_shape=(result, result), in_specs=[anywhe...  99 us
    pallas_call x1, Pallas kernels, fused_on_device(): pl.pallas_call(place_kernel, out_shape=(result, result), in_specs=[anywhe...  2.51 us

profile of v5, /device:TPU:28, one launch (start us, length us, event | category | flops | bytes accessed | tf_op | source)
XLA Modules:
  0.0 102.2 jit_solution(17043673618856528429)
XLA Ops:
  0.6 99.0 %layer.1 = (bf16[512,640]{1,0:T(8,128)(2,1)}, bf16[512,640]{1,0:T(8,128)(2,1)}) custom-call(bf16[512,640]{1,0:T(8,128)(2,1)} %tok.1, bf16[512,640]{1,0:T(8,128)(2,1)} %tan.1, f32[20,512]{1,0:T(8,128)} %bitcast.3, f32[20,512]{1,0:T(8,128)} %bitcast.4, bf16[2560,1280]{1,0:T(8,128)(2,1)} %w_in.1, bf16[2560,128]{1,0:T(8,128)(2,1)} %w_b.1, ...), custom_call_target="tpu_custom_call" | custom-call | tf_op jit(solution)/shard_map/layer/pallas_call | solution.py:633
  99.7 2.5 %place.1 = (bf16[512,640]{1,0:T(8,128)(2,1)}, bf16[512,640]{1,0:T(8,128)(2,1)}) custom-call(bf16[512,640]{1,0:T(8,128)(2,1)} %get-tuple-element.4.values, bf16[512,640]{1,0:T(8,128)(2,1)} %get-tuple-element.5.values_dot), custom_call_target="tpu_custom_call" | custom-call | tf_op jit(solution)/shard_map/place/pallas_call | solution.py:690
